TPU v7x, 512 devices: a whole 4x4x16 slice. The times are simulated.
512 devices in a mesh: lat: 8 (over y, z_hi), lon: 64 (over z_lo, x, core).
Axes of the slice: x: 4, y: 4, z: 16 (z_hi: 2, z_lo: 8; z = z_hi * 8 + z_lo), core: 2. Of those that a mesh axis runs over, the one named last changes fastest.
Arguments:
- inputs: bfloat16 [2, 48, 768, 192], P(None, 'lat', 'lon'), may hold values from -6 to 6
- cotangent: bfloat16 [2, 48, 768, 192], P(None, 'lat', 'lon'), may hold values from -6 to 6
- gains: float32 [2, 192], replicated, may hold values from 0.5 to 1.5
- qkv_weights: bfloat16 [2, 192, 576], replicated, may hold values from -0.4375 to 0.4375
- proj_weights: bfloat16 [2, 192, 192], replicated, may hold values from -0.4375 to 0.4375
- bias_tables: float32 [2, 8, 6, 23, 144], P(None, 'lat'), may hold values from -4 to 340
- pad_rows: int32 [48], replicated, may hold values 0 or 1
Outputs:
- outputs: bfloat16 [2, 48, 768, 192], P(None, 'lat', 'lon')
- d_inputs: bfloat16 [2, 48, 768, 192], P(None, 'lat', 'lon')
- d_gains: float32 [2, 192], replicated
- d_qkv: float32 [2, 192, 576], replicated
- d_proj: float32 [2, 192, 192], replicated
- d_tables: float32 [2, 8, 6, 23, 144], P(None, 'lat')
All inputs are finite; a program needn't handle non-finite values.
Results may differ from a plain program's by a relative error of at most 0.015.
Values may be sent and summed in bfloat16 or wider, within the bound.
A program may use at most 64 MiB of HBM per device.

v0:
```python
import jax
import jax.numpy as jnp
import numpy as np
from jax import lax
from jax.sharding import PartitionSpec as P


def shifted(value, axis, by):
    devices = lax.axis_size(axis)
    return lax.ppermute(value, axis, [(i, (i + by) % devices) for i in range(devices)])


def offset_table():
    distance = np.arange(23)[:, None, None]
    query_col = np.arange(12)[None, :, None]
    key_col = np.arange(12)[None, None, :]
    return jnp.asarray((key_col - query_col + 11 == distance).astype(np.float32))


def product(form, left, right):
    return jnp.einsum(form, left, right, preferred_element_type=jnp.float32)


def to_windows(field):
    level_count, row_count, col_count = field.shape[:3]
    remain = field.shape[3:]
    shaped = field.reshape((level_count, row_count // 6, 6, col_count // 12, 12) + remain)
    order = (1, 3, 0, 2, 4) + tuple(range(5, 5 + len(remain)))
    return shaped.transpose(order).reshape(
        (row_count // 6, col_count // 12, level_count * 72) + remain
    )


def from_windows(windows, level_count, row_count, col_count):
    remain = windows.shape[3:]
    shaped = windows.reshape((row_count // 6, col_count // 12, level_count, 6, 12) + remain)
    order = (2, 0, 3, 1, 4) + tuple(range(5, 5 + len(remain)))
    return shaped.transpose(order).reshape((level_count, row_count, col_count) + remain)


def shifted_regions(level_count, row_count, col_count, row_start, total_rows):
    rows = row_start + jnp.arange(row_count, dtype=jnp.int32)
    band = (rows >= total_rows - 6).astype(jnp.int32) + (rows >= total_rows - 3).astype(jnp.int32)
    levels = 3 * jnp.arange(level_count, dtype=jnp.int32)
    ids = levels[:, None] + band[None, :]
    return jnp.broadcast_to(ids[:, :, None], (level_count, row_count, col_count))


def expand_bias(table):
    window_count, head_count = table.shape[:2]
    divided = table.reshape(window_count, head_count, 23, 2, 2, 6, 6)
    full = jnp.einsum(
        "thdabce,dfg->thacfbeg", divided, offset_table(), precision=lax.Precision.HIGHEST
    )
    return full.reshape(window_count, head_count, 144, 144)


def fold_bias(grads):
    window_count, head_count = grads.shape[:2]
    divided = grads.reshape(window_count, head_count, 2, 6, 12, 2, 6, 12)
    folded = jnp.einsum(
        "thacfbeg,dfg->thdabce", divided, offset_table(), precision=lax.Precision.HIGHEST
    )
    return folded.reshape(window_count, head_count, 23, 144)


def attend_forward(hidden, gain, w_qkv, w_proj, bias, allowed):
    head_count = bias.shape[1]
    feature_count = hidden.shape[-1]
    head_size = feature_count // head_count
    score_scale = head_size ** (-0.5)
    values = hidden.astype(jnp.float32)
    center = values - jnp.mean(values, -1, keepdims=True)
    inverse = lax.rsqrt(jnp.mean(center * center, -1, keepdims=True) + 1e-05)
    normed = center * inverse
    scaled = (normed * gain).astype(jnp.bfloat16)
    packed = product("absc,cf->absf", scaled, w_qkv).astype(jnp.bfloat16)
    divided = packed.reshape(packed.shape[:3] + (3, head_count, head_size))
    query_part = divided[:, :, :, 0]
    key_part = divided[:, :, :, 1]
    value_part = divided[:, :, :, 2]
    scores = product("abqhd,abkhd->abhqk", query_part, key_part) * score_scale + bias[:, None]
    permit = allowed[:, :, None]
    scores = jnp.where(permit, scores, -1e30)
    row_max = jnp.max(scores, -1, keepdims=True)
    weight = jnp.where(permit, jnp.exp(scores - row_max), 0.0)
    attention = weight / jnp.sum(weight, -1, keepdims=True)
    rounded = attention.astype(jnp.bfloat16)
    mixture = (
        product("abhqk,abkhd->abqhd", rounded, value_part)
        .astype(jnp.bfloat16)
        .reshape(hidden.shape)
    )
    output = (values + product("absc,cf->absf", mixture, w_proj)).astype(jnp.bfloat16)
    return (
        output,
        (normed, inverse, scaled, query_part, key_part, value_part, attention, rounded, mixture),
    )


def attend_backward(incoming, saved, gain, w_qkv, w_proj):
    normed, inverse, scaled, query_part, key_part, value_part, attention, rounded, mixture = saved
    head_count, head_size = query_part.shape[-2:]
    score_scale = head_size ** (-0.5)
    d_proj = product("absc,absf->cf", mixture, incoming)
    back_grad = product("absf,cf->absc", incoming, w_proj).astype(jnp.bfloat16)
    back_grad = back_grad.reshape(back_grad.shape[:3] + (head_count, head_size))
    d_attention = product("abqhd,abkhd->abhqk", back_grad, value_part)
    d_values = product("abhqk,abqhd->abkhd", rounded, back_grad).astype(jnp.bfloat16)
    d_scores = attention * (d_attention - jnp.sum(d_attention * attention, -1, keepdims=True))
    d_bias = jnp.sum(d_scores, 1)
    d_rounded = (d_scores * score_scale).astype(jnp.bfloat16)
    d_query = product("abhqk,abkhd->abqhd", d_rounded, key_part).astype(jnp.bfloat16)
    d_keys = product("abhqk,abqhd->abkhd", d_rounded, query_part).astype(jnp.bfloat16)
    d_packed = jnp.stack([d_query, d_keys, d_values], 3).reshape(
        incoming.shape[:3] + (w_qkv.shape[1],)
    )
    d_qkv = product("absc,absf->cf", scaled, d_packed)
    d_scaled = product("absf,cf->absc", d_packed, w_qkv)
    d_gain = jnp.sum(d_scaled * normed, (0, 1, 2))
    d_normed = d_scaled * gain
    d_hidden = inverse * (
        d_normed
        - jnp.mean(d_normed, -1, keepdims=True)
        - normed * jnp.mean(d_normed * normed, -1, keepdims=True)
    )
    result = (incoming.astype(jnp.float32) + d_hidden).astype(jnp.bfloat16)
    return (result, d_gain, d_qkv, d_proj, d_bias)


def roll_frame(field, direction):
    if direction < 0:
        col_edge = field[:, :, :6]
    else:
        col_edge = field[:, :, -6:]
    arrived = shifted(col_edge, "lon", direction)
    if direction < 0:
        field = jnp.concatenate([field[:, :, 6:], arrived], 2)
    else:
        field = jnp.concatenate([arrived, field[:, :, :-6]], 2)
    if direction < 0:
        row_edge = field[:, :3]
    else:
        row_edge = field[:, -3:]
    landed = shifted(row_edge, "lat", direction)
    if direction < 0:
        field = jnp.concatenate([field[:, 3:], landed], 1)
    else:
        field = jnp.concatenate([landed, field[:, :-3]], 1)
    return jnp.roll(field, direction, axis=0)


def body(inputs, cotangent, gains, qkv_weights, proj_weights, bias_tables, pad_rows):
    level_count, row_count, col_count = inputs.shape[:3]
    diagonal = jnp.eye(144, dtype=bool)
    row_start = lax.axis_index("lat") * row_count
    total_rows = row_count * lax.axis_size("lat")
    plain_rows = lax.dynamic_slice_in_dim(pad_rows, row_start, row_count) == 1
    extended = jnp.concatenate([pad_rows, pad_rows[:3]])
    moved_rows = lax.dynamic_slice_in_dim(extended, row_start + 3, row_count) == 1

    def key_valid(rows_ok):
        field = jnp.broadcast_to(rows_ok[None, :, None], (level_count, row_count, col_count))
        return to_windows(field)[:, :, None, :]

    allow_first = key_valid(plain_rows) | diagonal
    regions = to_windows(shifted_regions(level_count, row_count, col_count, row_start, total_rows))
    allow_second = (regions[:, :, :, None] == regions[:, :, None, :]) & (
        key_valid(moved_rows) | diagonal
    )
    bias_first = expand_bias(bias_tables[0])
    bias_second = expand_bias(bias_tables[1])
    first, saved_first = attend_forward(
        to_windows(inputs), gains[0], qkv_weights[0], proj_weights[0], bias_first, allow_first
    )
    first_field = from_windows(first, level_count, row_count, col_count)
    second, saved_second = attend_forward(
        to_windows(roll_frame(first_field, -1)),
        gains[1],
        qkv_weights[1],
        proj_weights[1],
        bias_second,
        allow_second,
    )
    outputs = roll_frame(from_windows(second, level_count, row_count, col_count), 1)
    incoming = to_windows(roll_frame(cotangent, -1))
    back_second = attend_backward(incoming, saved_second, gains[1], qkv_weights[1], proj_weights[1])
    pieces_second = tuple(back_second[1:4]) + (fold_bias(back_second[4]),)
    returned = to_windows(
        roll_frame(from_windows(back_second[0], level_count, row_count, col_count), 1)
    )
    back_first = attend_backward(returned, saved_first, gains[0], qkv_weights[0], proj_weights[0])
    grad_windows = back_first[0]
    pieces_first = tuple(back_first[1:4]) + (fold_bias(back_first[4]),)
    stacked = tuple(
        (
            jnp.stack([first_part, second_part])
            for first_part, second_part in zip(pieces_first, pieces_second)
        )
    )
    weight_totals = lax.psum((stacked[0], stacked[1], stacked[2]), ("lat", "lon"))
    table_total = lax.psum(stacked[3], "lon")
    totals = tuple(weight_totals) + (table_total,)
    d_inputs = from_windows(grad_windows, level_count, row_count, col_count)
    return (outputs, d_inputs, totals[0], totals[1], totals[2], totals[3])


def solution(mesh):
    placed = (
        P(None, "lat", "lon", None),
        P(None, "lat", "lon", None),
        P(),
        P(),
        P(),
        P(None, "lat", None, None, None),
        P(),
    )
    return jax.shard_map(
        body,
        mesh=mesh,
        in_specs=placed,
        out_specs=(
            P(None, "lat", "lon", None),
            P(None, "lat", "lon", None),
            P(),
            P(),
            P(),
            P(None, "lat", None, None, None),
        ),
        check_vma=False,
    )
```

profile of v0, /device:TPU:1, one launch (start us, length us, event | category | flops | bytes accessed | tf_op | source)
XLA Modules:
  0.0 1498.2 jit_solution(1736768366656291032)
XLA Ops:
  10.6 1.1 multiply_convert_fusion.7
  11.8 1.2 convolution_convert_fusion.1
  13.2 1.2 fusion.91
  14.7 8.5 convolution_bitcast_fusion.1
  23.2 11.3 copy.207
  34.5 5.0 reshape.882
  40.3 1.2 fusion.99
  43.3 8.8 collective-permute-start
  52.2 9.6 collective-permute-start.4
  63.4 7.6 convolution_bitcast_fusion
  71.0 11.3 copy.208
  82.4 5.0 reshape.884
  87.4 10.4 collective-permute-start.1
  98.5 6.0 collective-permute-start.5
  106.5 1.3 fusion.15
  107.8 2.0 fusion.100
  109.8 1.9 convolution_convert_fusion.8
  115.1 2.0 fusion.22
  117.1 1.2 fusion.54
  118.3 2.8 fusion.21
  121.1 2.5 fusion.20
  123.6 1.1 pad_maximum_fusion.2
  125.8 1.1 fusion.19
  126.9 1.0 convolution_bitcast_fusion.6
  128.0 3.1 fusion.11
  131.8 1.9 collective-permute-start.2
  134.5 2.1 collective-permute-start.6
  136.7 5.9 reshape.886
  142.6 11.0 copy.188
  153.6 11.6 convolution_bitcast_fusion.2
  167.4 7.4 collective-permute-start.7
  175.5 5.3 collective-permute-start.3
  180.8 2.5 collective-permute-done.7
  184.2 1.1 convolution_convert_fusion.10
  185.4 1.2 fusion.25
  186.9 1.3 fusion.24
  188.2 1.2 fusion.23
  189.6 1.9 multiply_reduce_fusion.3
  191.7 2.6 fusion.13
  195.4 5.9 reshape.885
  201.3 11.0 copy.185
  212.4 11.6 convolution_bitcast_fusion.3
  229.3 106.9 %psum.28 = f32[2,192]{1,0:T(2,128)} all-reduce(f32[2,192]{1,0:T(2,128)S(1)} %pad_maximum_fusion.13), channel_id=1, replica_groups=mesh['lat'=8,'lon'=64] {'lat','lon'}, use_global_device_ids=true, to_apply=%region_16.17 | all-reduce | flops 384 | bytes 3072 | tf_op jit(solution)/shard_map/psum | solution.py:201
  336.3 673.5 %all-reduce.4.cloned.1.call-done = f32[2,1,6,23,144]{4,0,3,2,1:T(2,128)} async-done(((f32[2,1,6,23,144]{4,0,3,2,1:T(2,128)}), f32[2,1,6,23,144]{4,0,3,2,1:T(2,128)}) %all-reduce.4.cloned.1.call-update) | async-done | bytes 158992 | tf_op jit(solution)/shard_map/psum | solution.py:202
  1009.7 2.0 copy.194
  1011.7 475.7 %all-reduce.6.cloned.1.call-done = (f32[2,192,576]{2,1,0:T(8,128)}, f32[2,192,192]{2,1,0:T(8,128)}) async-done(((f32[2,192,576]{2,1,0:T(8,128)}, f32[2,192,192]{2,1,0:T(8,128)}), (f32[2,192,576]{2,1,0:T(8,128)}, f32[2,192,192]{2,1,0:T(8,128)})) %all-reduce.6.cloned.1.call-update) | async-done | bytes 1179664 | tf_op jit(solution)/shard_map/psum | solution.py:201
  1487.4 2.2 copy.221
  1489.6 1.8 copy.222
  (166 shorter events, 27.6 us)
Async XLA Ops:
  7.2 1002.6 %all-reduce.4.cloned.1.call-start = ((), (), s32[]{:S(2)}) async-start(), calls=%async_computation | async-start | bytes 565248 | tf_op jit(solution)/shard_map/psum | solution.py:202
  10.4 24.1 %copy-start.22 = (f32[144]{0:T(256)}, f32[144]{0:T(256)S(1)}, u32[]{:S(2)}) copy-start(f32[144]{0:T(256)S(1)} %add_rsqrt_fusion.1) | copy-start | bytes 1732
  11.8 2.6 copy-start.5
  34.5 5.0 copy-start.28
  34.5 8.0 copy-start.4
  34.5 17.6 %copy-start.21 = (bf16[2,6,12,192]{3,0,2,1:T(2,128)(2,1)S(1)}, bf16[2,6,12,192]{3,0,2,1:T(2,128)(2,1)}, u32[]{:S(2)}) copy-start(bf16[2,6,12,192]{3,0,2,1:T(2,128)(2,1)} %param.12) | copy-start | bytes 165892
  39.5 23.9 %copy-start.14 = (f32[23,12,12,1,1,1,1]{0,2,6,5,4,3,1:T(8,128)S(1)}, f32[23,12,12,1,1,1,1]{0,2,6,5,4,3,1:T(8,128)}, u32[]{:S(2)}) copy-start(f32[23,12,12,1,1,1,1]{0,2,6,5,4,3,1:T(8,128)} %constant.50) | copy-start | bytes 39748
  39.9 21.9 %copy-start.17 = (pred[144,144]{0,1:T(8,128)(4,1)}, pred[144,144]{0,1:T(8,128)(4,1)S(1)}, u32[]{:S(2)}) copy-start(pred[144,144]{0,1:T(8,128)(4,1)S(1)} %fusion.43) | copy-start | bytes 62212
  41.4 1.9 copy-start.26
  41.8 0.7 copy-start.15
  43.3 44.0 %collective-permute-start = (bf16[2,6,6,192]{3,2,1,0:T(8,128)(2,1)}, bf16[2,6,6,192]{3,2,1,0:T(8,128)(2,1)S(1)}, u32[]{:S(2)}, u32[]{:S(2)}) collective-permute-start(bf16[2,6,6,192]{3,2,1,0:T(8,128)(2,1)} %get-tuple-element.57), channel_id=1, source_target_pairs={{0,63},{1,0},{2,1},{3,2},{4,3},{5,4},{6,5},{7,6},{8,7},{9,8},{10,9... | collective-permute-start | bytes 82952 | tf_op jit(solution)/shard_map/ppermute | solution.py:10
  52.2 45.6 %collective-permute-start.4 = (bf16[2,6,6,192]{3,0,2,1:T(2,128)(2,1)S(1)}, bf16[2,6,6,192]{3,0,2,1:T(2,128)(2,1)S(1)}, u32[]{:S(2)}, u32[]{:S(2)}) collective-permute-start(bf16[2,6,6,192]{3,0,2,1:T(2,128)(2,1)S(1)} %get-tuple-element.61), channel_id=1, source_target_pairs={{0,63},{1,0},{2,1},{3,2},{4,3},{5,4},{6,5},{7,6},{8,7},{9,8},{10,9... | collective-permute-start | bytes 82952 | tf_op jit(solution)/shard_map/ppermute | solution.py:10
  82.3 23.0 %copy-start.10 = (bf16[2,192,576]{2,1,0:T(8,128)(2,1)S(1)}, bf16[2,192,576]{2,1,0:T(8,128)(2,1)}, u32[]{:S(2)}) copy-start(bf16[2,192,576]{2,1,0:T(8,128)(2,1)} %param.14) | copy-start | bytes 1327108
  87.4 17.2 %collective-permute-start.1 = (bf16[2,3,12,192]{3,2,1,0:T(8,128)(2,1)S(1)}, bf16[2,3,12,192]{3,2,1,0:T(8,128)(2,1)S(1)}, u32[]{:S(2)}, u32[]{:S(2)}) collective-permute-start(bf16[2,3,12,192]{3,2,1,0:T(8,128)(2,1)S(1)} %get-tuple-element.55), channel_id=1, source_target_pairs={{0,448},{64,0},{128,64},{192,128},{256,192},{320,256},{384,320},{4... | collective-permute-start | bytes 82952 | tf_op jit(solution)/shard_map/ppermute | solution.py:10
  98.5 13.7 collective-permute-start.5
  105.1 19.8 %copy-start.24 = (f32[144]{0:T(256)}, f32[144]{0:T(256)S(1)}, u32[]{:S(2)}) copy-start(f32[144]{0:T(256)S(1)} %add_rsqrt_fusion) | copy-start | bytes 1732
  105.4 1.1 copy-start.7
  107.8 9.3 copy-start
  115.1 9.5 copy-start.8
  115.1 9.8 copy-start.11
  118.3 2.8 copy-start.2
  125.8 7.9 copy-start.25
  131.8 43.1 %collective-permute-start.2 = (bf16[2,6,6,192]{3,2,1,0:T(8,128)(2,1)}, bf16[2,6,6,192]{3,2,1,0:T(8,128)(2,1)S(1)}, u32[]{:S(2)}, u32[]{:S(2)}) collective-permute-start(bf16[2,6,6,192]{3,2,1,0:T(8,128)(2,1)} %get-tuple-element.52), channel_id=1, source_target_pairs={{0,1},{1,2},{2,3},{3,4},{4,5},{5,6},{6,7},{7,8},{8,9},{9,10},{10,1... | collective-permute-start | bytes 82952 | tf_op jit(solution)/shard_map/ppermute | solution.py:10
  134.5 32.2 %collective-permute-start.6 = (bf16[2,6,6,192]{3,2,1,0:T(8,128)(2,1)}, bf16[2,6,6,192]{3,2,1,0:T(8,128)(2,1)}, u32[]{:S(2)}, u32[]{:S(2)}) collective-permute-start(bf16[2,6,6,192]{3,2,1,0:T(8,128)(2,1)} %get-tuple-element.48), channel_id=1, source_target_pairs={{0,1},{1,2},{2,3},{3,4},{4,5},{5,6},{6,7},{7,8},{8,9},{9,10},{10,1... | collective-permute-start | bytes 82952 | tf_op jit(solution)/shard_map/ppermute | solution.py:10
  142.6 11.0 copy-start.12
  153.6 33.3 %copy-start.1 = (f32[6,144,144]{1,2,0:T(8,128)S(1)}, f32[6,144,144]{1,2,0:T(8,128)}, u32[]{:S(2)}) copy-start(f32[6,144,144]{1,2,0:T(8,128)} %get-tuple-element.65) | copy-start | bytes 1492996
  167.4 15.9 %collective-permute-start.7 = (bf16[2,3,12,192]{3,2,1,0:T(8,128)(2,1)S(1)}, bf16[2,3,12,192]{3,2,1,0:T(8,128)(2,1)S(1)}, u32[]{:S(2)}, u32[]{:S(2)}) collective-permute-start(bf16[2,3,12,192]{3,2,1,0:T(8,128)(2,1)S(1)} %fusion.76), channel_id=1, source_target_pairs={{0,64},{64,128},{128,192},{192,256},{256,320},{320,384},{384,448},... | collective-permute-start | bytes 82952 | tf_op jit(solution)/shard_map/ppermute | solution.py:10
  174.9 8.4 copy-start.18
  175.5 19.0 %collective-permute-start.3 = (bf16[2,3,12,192]{3,2,1,0:T(8,128)(2,1)}, bf16[2,3,12,192]{3,2,1,0:T(8,128)(2,1)}, u32[]{:S(2)}, u32[]{:S(2)}) collective-permute-start(bf16[2,3,12,192]{3,2,1,0:T(8,128)(2,1)} %fusion.77), channel_id=1, source_target_pairs={{0,64},{64,128},{128,192},{192,256},{256,320},{320,384},{384,448},... | collective-permute-start | bytes 82952 | tf_op jit(solution)/shard_map/ppermute | solution.py:10
  185.4 4.2 copy-start.23
  185.4 6.0 copy-start.6
  186.9 1.3 copy-start.3
  188.2 6.1 copy-start.16
  188.2 6.3 copy-start.19
  201.3 11.0 copy-start.13
  212.4 12.4 copy-start.9
  212.4 16.1 %copy-start.20 = (f32[144,192]{1,0:T(8,128)S(1)}, f32[144,192]{1,0:T(8,128)}, u32[]{:S(2)}) copy-start(f32[144,192]{1,0:T(8,128)} %get-tuple-element.69) | copy-start | bytes 331780
  212.4 17.0 %copy-start.27 = (f32[192]{0:T(256)S(1)}, f32[192]{0:T(256)}, u32[]{:S(2)}) copy-start(f32[192]{0:T(256)} %get-tuple-element.38) | copy-start | bytes 2308
  225.8 1261.5 %all-reduce.6.cloned.1.call-start = ((), (), s32[]{:S(2)}) async-start(), calls=%async_computation.1 | async-start | bytes 2752512 | tf_op jit(solution)/shard_map/psum | solution.py:201
Sparse Core Ops, SparseCore 0:
  226.0 783.7 all-reduce.3
  1016.7 470.6 all-reduce.5
where the time goes:
time: 1500 us
  waiting for transfers between devices  1150 us (77%)
  blocking collectives  107 us (7%)
  local copies, waits for them, and re-layouts  85.6 us (6%)
  matrix products  64.1 us (4%)
  starting transfers between devices  51.6 us (3%)
  other arithmetic  22.8 us (2%)
    psum x1, waiting for transfers between devices, body(): table_total = lax.psum(stacked[3], 'lon')  673 us
    psum x1, waiting for transfers between devices, body(): lax.psum((stacked[0], stacked[1], stacked[2]), ('lat', 'lon'))  476 us
    psum x1, blocking collectives, body(): lax.psum((stacked[0], stacked[1], stacked[2]), ('lat', 'lon'))  107 us
    ppermute x8, starting transfers between devices, shifted(): lax.ppermute(value, axis, [(i, (i + by) % devices) for i in range(devices)])  51.5 us
    another operation x6, local copies, waits for them, and re-layouts  34 us
    another operation x4, local copies, waits for them, and re-layouts, attend_forward(): bias[:, None]  32.6 us
  transfers between devices with their start and end apart: 10, of which 4 were waited for; matrix products, arithmetic and copies ran while one was open for 5% of the time, Pallas kernels for 0%

commit v1 on v0

v1 whole, which is shorter than its diff:
```python
import jax
import jax.numpy as jnp
import numpy as np
from jax import lax
from jax.experimental import pallas as pl
from jax.experimental.pallas import tpu as pltpu
from jax.sharding import PartitionSpec as P

F32 = jnp.float32
BF16 = jnp.bfloat16
MESH = pl.DeviceIdType.MESH
HEADS = 6
SCALE = 32 ** (-0.5)


def orders():
    pos_a = np.zeros((2, 6, 12), np.int64)
    pos_n = np.zeros((2, 6, 12), np.int64)
    pos_b = np.zeros((2, 6, 12), np.int64)
    slot = np.zeros((2, 6, 12), np.int64)
    for l in range(2):
        for r in range(6):
            for c in range(12):
                pos_n[l, r, c] = l * 72 + r * 12 + c
                pos_a[l, r, c] = c * 12 + l * 6 + r
                pos_b[l, r, c] = l * 72 + c * 6 + r
                quarter = (r // 3) * 2 + c // 6
                slot[l, r, c] = quarter * 48 + l * 18 + (r % 3) * 6 + c % 6
    return pos_n.ravel(), pos_a.ravel(), pos_b.ravel(), slot.ravel()


def one_hot(rows, cols, shape):
    out = np.zeros(shape, np.float32)
    out[rows, cols] = 1.0
    return out


def constants():
    pos_n, pos_a, pos_b, slot = orders()
    perm = np.stack([one_hot(pos_a, pos_n, (144, 144)), one_hot(pos_n, pos_a, (144, 144))])
    to_slot = np.stack([one_hot(slot, p, (192, 144)) for p in (pos_n, pos_a, pos_b)])
    from_slot = np.stack([one_hot(p, slot, (144, 192)) for p in (pos_n, pos_a, pos_b)])
    exp1 = np.zeros((2, 3, 3, 24, 1024), np.float32)
    exp2 = np.zeros((2, 3, 3, 24, 512), np.float32)
    for par in range(2):
        for h in range(3):
            for o in range(23):
                start = 144 * par + 288 * h + (22 - o) * 12
                exp1[par, h, :, o, start : start + 12] = 1.0
                start = 72 * par + 144 * h + (22 - o) * 6
                exp2[par, h, :, o, start : start + 6] = 1.0
    lanes = np.arange(1024)
    info = np.zeros((8, 1024), np.int32)
    info[0] = lanes % 12
    info[1] = lanes % 144
    info[2] = (lanes // 144) % 2 + 2 * (lanes >= 864)
    info[3] = lanes % 6
    info[4] = lanes % 72
    info[5] = (lanes // 72) % 2 + 2 * (lanes >= 432)
    return (
        jnp.asarray(perm, BF16),
        jnp.asarray(to_slot, BF16),
        jnp.asarray(from_slot, BF16),
        jnp.asarray(exp1.reshape(2, 216, 1024), BF16),
        jnp.asarray(exp2.reshape(2, 216, 512), BF16),
        jnp.asarray(exp1[:, :, 0].reshape(2, 72, 1024), BF16),
        jnp.asarray(exp2[:, :, 0].reshape(2, 72, 512), BF16),
        jnp.asarray(info),
    )


def nn(a, b):
    return lax.dot_general(a, b, (((1,), (0,)), ((), ())), preferred_element_type=F32)


def nt(a, b):
    return lax.dot_general(a, b, (((1,), (1,)), ((), ())), preferred_element_type=F32)


def tn(a, b):
    return lax.dot_general(a, b, (((0,), (0,)), ((), ())), preferred_element_type=F32)


def head_stack(x):
    lane = lax.broadcasted_iota(jnp.int32, (1, 192), 1)
    parts = [jnp.where((lane >= 32 * h) & (lane < 32 * h + 32), x, 0.0) for h in range(HEADS)]
    return jnp.concatenate(parts, 0).astype(BF16)


def head_diagonal(x, n):
    return jnp.concatenate(
        [x[32 * h : 32 * h + 32, n * h : n * h + n] for h in range(HEADS)], 0
    )


def split_table(s, tab_ref, block):
    out = []
    for h in range(HEADS):
        s.tab[h, 0:23, :] = tab_ref[block, 0, h]
    for par in range(2):
        parts = []
        for h in range(3):
            t = s.tab[2 * h + par]
            hi = t.astype(BF16).astype(F32)
            rest = t - hi
            mid = rest.astype(BF16).astype(F32)
            parts += [hi, mid, rest - mid]
        out.append(jnp.concatenate(parts, 0).astype(BF16))
    return out


def row_flags(pad_ref, start, total):
    rows = lax.broadcasted_iota(jnp.int32, (6, 1), 0)
    flags = jnp.zeros((6, 1), jnp.int32)
    for r in range(6):
        flags = jnp.where(rows == r, pad_ref[lax.rem(start + r, total)], flags)
    return rows, flags == 1


def expand_first(s, tab_ref, exp_ref, info_ref, pad_ref, lat):
    for par, parts in enumerate(split_table(s, tab_ref, 0)):
        s.wide[par] = tn(parts, exp_ref[par])
    l12 = info_ref[0:1, :]
    l144 = info_ref[1:2, 0:864]
    odd = info_ref[2:3, 0:864] == 1
    rows, valid = row_flags(pad_ref, 6 * lat, 48)
    for lk in range(2):
        strips = []
        for par in range(2):
            strip = jnp.zeros((6, 1024), F32)
            for e in range(12):
                at = 72 * (e // 6) + 36 * lk + 6 * (e % 6)
                strip = jnp.where(l12 == e, s.wide[par, at : at + 6, :], strip)
            strips.append(strip)
        for ck in range(12):
            turn = (1024 - (11 - ck) * 12) % 1024
            even_part, odd_part = [
                (pltpu.roll(x, turn, 1) if turn else x)[:, 0:864] for x in strips
            ]
            at = 12 * ck + 6 * lk
            keep = valid | (l144 == rows + at)
            s.bias1[at : at + 6, :] = jnp.where(
                keep, jnp.where(odd, odd_part, even_part), -1e30
            )


def expand_second(s, tab_ref, exp_ref, info_ref, pad_ref, lat):
    for par, parts in enumerate(split_table(s, tab_ref, 1)):
        s.wide[par, :, 0:512] = tn(parts, exp_ref[par])
    l6 = info_ref[3:4, 0:512]
    l72 = info_ref[4:5, 0:432]
    odd = info_ref[5:6, 0:432] == 1
    rows, valid = row_flags(pad_ref, 6 * lat + 3, 48)
    q_band = jnp.where(lat == 7, (info_ref[3:4, 0:432] >= 3).astype(jnp.int32), 0)
    k_band = jnp.where(lat == 7, (rows >= 3).astype(jnp.int32), 0)
    same = q_band == k_band
    for lev in range(2):
        strips = []
        for par in range(2):
            strip = jnp.zeros((6, 512), F32)
            for e in range(6):
                at = 108 * (1 - lev) + 6 * e
                strip = jnp.where(l6 == e, s.wide[par, at : at + 6, 0:512], strip)
            strips.append(strip)
        for ck in range(12):
            turn = (512 - (11 - ck) * 6) % 512
            even_part, odd_part = [
                (pltpu.roll(x, turn, 1) if turn else x)[:, 0:432] for x in strips
            ]
            at = 6 * ck
            keep = (valid | (l72 == rows + at)) & same
            s.bias2[lev, at : at + 6, :] = jnp.where(
                keep, jnp.where(odd, odd_part, even_part), -1e30
            )


def fold_first(s, one_ref, info_ref):
    l12 = info_ref[0:1, :]
    for par in range(2):
        mine = info_ref[2:3, :] == par
        for lk in range(2):
            acc = jnp.zeros((6, 1024), F32)
            for ck in range(12):
                at = 12 * ck + 6 * lk
                piece = jnp.where(mine, s.ds[at : at + 6, :], 0.0)
                turn = (11 - ck) * 12
                acc = acc + (pltpu.roll(piece, turn, 1) if turn else piece)
            for e in range(12):
                at = 72 * (e // 6) + 36 * lk + 6 * (e % 6)
                s.wide[par, at : at + 6, :] = jnp.where(l12 == e, acc, 0.0)
    return [nt(one_ref[par], s.wide[par].astype(BF16)) for par in range(2)]


def fold_second(s, one_ref, info_ref):
    l6 = info_ref[3:4, 0:512]
    s.wide[:, :, 0:512] = jnp.zeros((2, 144, 512), F32)
    for par in range(2):
        mine = info_ref[5:6, 0:512] == par
        for lev in range(2):
            acc = jnp.zeros((6, 512), F32)
            for ck in range(12):
                at = 72 * lev + 6 * ck
                piece = jnp.where(mine, s.ds[at : at + 6, 0:512], 0.0)
                turn = (11 - ck) * 6
                acc = acc + (pltpu.roll(piece, turn, 1) if turn else piece)
            for e in range(6):
                at = 108 * (1 - lev) + 6 * e
                s.wide[par, at : at + 6, 0:512] = jnp.where(l6 == e, acc, 0.0)
    return [nt(one_ref[par], s.wide[par, :, 0:512].astype(BF16)) for par in range(2)]


def forward(s, j, x, gain, wqkv_ref, wproj_ref, bias, groups):
    n = 144 // groups
    center = x - jnp.mean(x, -1, keepdims=True)
    inverse = lax.rsqrt(jnp.mean(center * center, -1, keepdims=True) + 1e-05)
    normed = center * inverse
    scaled = (normed * gain).astype(BF16)
    packed = nn(scaled, wqkv_ref[j])
    q, k, v = packed[:, 0:192], packed[:, 192:384], packed[:, 384:576]
    s.normed[j] = normed
    s.inverse[j] = inverse
    s.scaled[j] = scaled
    s.k[j] = k
    s.v[j] = v
    attended = []
    for g in range(groups):
        rows = slice(g * n, g * n + n)
        qm = head_stack(q[rows])
        s.qm[j, g * 6 * n : (g + 1) * 6 * n, :] = qm
        scores = nt(k[rows].astype(BF16), qm) * SCALE + bias(g)
        weight = jnp.exp(scores - jnp.max(scores, 0, keepdims=True))
        probs = weight * (1.0 / jnp.sum(weight, 0, keepdims=True))
        s.probs[j, rows, 0 : 6 * n] = probs
        mixed_t = head_diagonal(tn(v[rows].astype(BF16), probs.astype(BF16)), n)
        s.mixed_t[j, g, :, 0:n] = mixed_t
        attended.append(tn(mixed_t.astype(BF16), wproj_ref[j]))
    att = attended[0] if groups == 1 else jnp.concatenate(attended, 0)
    return (x + att).astype(BF16)


def backward(s, j, g_in, gain, wqkv_ref, wproj_ref, groups):
    n = 144 // groups
    back = nt(g_in, wproj_ref[j])
    dqs, dks, dvs = [], [], []
    for g in range(groups):
        rows = slice(g * n, g * n + n)
        backm = head_stack(back[rows])
        probs = s.probs[j, rows, 0 : 6 * n]
        k = s.k[j, rows, :].astype(BF16)
        v = s.v[j, rows, :].astype(BF16)
        qm = s.qm[j, g * 6 * n : (g + 1) * 6 * n, :]
        d_probs = nt(v, backm)
        dvs.append(nn(probs.astype(BF16), backm))
        d_scores = probs * (d_probs - jnp.sum(d_probs * probs, 0, keepdims=True))
        s.ds[rows, 0 : 6 * n] = d_scores
        d_rounded = (d_scores * SCALE).astype(BF16)
        dks.append(nn(d_rounded, qm))
        dqs.append(head_diagonal(tn(k, d_rounded), n).T)
    if groups == 1:
        dq, dk, dv = dqs[0], dks[0], dvs[0]
    else:
        dq, dk, dv = [jnp.concatenate(p, 0) for p in (dqs, dks, dvs)]
    dq, dk, dv = dq.astype(BF16), dk.astype(BF16), dv.astype(BF16)
    w = wqkv_ref[j]
    d_scaled = nt(dq, w[:, 0:192]) + nt(dk, w[:, 192:384]) + nt(dv, w[:, 384:576])
    normed = s.normed[j]
    d_normed = d_scaled * gain
    d_hidden = s.inverse[j] * (
        d_normed
        - jnp.mean(d_normed, -1, keepdims=True)
        - normed * jnp.mean(d_normed * normed, -1, keepdims=True)
    )
    result = (g_in.astype(F32) + d_hidden).astype(BF16)
    return result, (dq, dk, dv, d_scaled)


def gradients(s, j, g_in, saved, folded, groups):
    n = 144 // groups
    dq, dk, dv, d_scaled = saved
    scaled = s.scaled[j]
    s.grad[:, 0:192] = tn(scaled, dq)
    s.grad[:, 192:384] = tn(scaled, dk)
    s.grad[:, 384:576] = tn(scaled, dv)
    d_proj = jnp.zeros((192, 192), F32)
    for g in range(groups):
        d_proj = d_proj + nn(
            s.mixed_t[j, g, :, 0:n].astype(BF16), g_in[g * n : g * n + n]
        )
    s.grad[:, 576:768] = d_proj
    for c in range(6):
        s.send[j, c] = s.grad[:, 128 * c : 128 * c + 128].astype(BF16)
    for h in range(HEADS):
        s.extra[24 * h : 24 * h + 24, 0:144] = folded[h % 2][24 * (h // 2) : 24 * (h // 2) + 24]
    s.extra[144:145, 0:192] = jnp.sum(d_scaled * s.normed[j], 0, keepdims=True)
    for c in range(2):
        s.send[j, 6 + c] = s.extra[:, 128 * c : 128 * c + 128].astype(BF16)


class Halo:
    def __init__(self, s, which, forward_shift):
        lat, lon = lax.axis_index("lat"), lax.axis_index("lon")
        nlat, nlon = lax.axis_size("lat"), lax.axis_size("lon")
        self.s, self.which = s, which
        self.copies = []
        self.stay = 3 if forward_shift else 0
        for i, quarter in enumerate(q for q in range(4) if q != self.stay):
            if forward_shift:
                by_lat, by_lon = quarter // 2 - 1 + nlat, quarter % 2 - 1 + nlon
            else:
                by_lat, by_lon = quarter // 2, quarter % 2
            self.copies.append(
                pltpu.make_async_remote_copy(
                    src_ref=s.halo_out.at[which, quarter],
                    dst_ref=s.halo_in.at[which, 3 - quarter],
                    send_sem=s.halo_send.at[which, i],
                    recv_sem=s.halo_recv.at[which, i],
                    device_id=(lax.rem(lat + by_lat, nlat), lax.rem(lon + by_lon, nlon)),
                    device_id_type=MESH,
                )
            )

    def start(self, quarters):
        for q in range(4):
            self.s.halo_out[self.which, q] = quarters[48 * q : 48 * q + 48]
        for copy in self.copies:
            copy.start()
        stay = self.stay
        self.s.halo_in[self.which, 3 - stay] = quarters[48 * stay : 48 * stay + 48]

    def finish(self):
        for copy in self.copies:
            copy.wait()
        return jnp.concatenate([self.s.halo_in[self.which, q] for q in range(4)], 0)


class Stage:
    def __init__(self, s, j, number, me, peer_id, src, dst):
        self.copies = []
        for d in range(1, 8):
            peer = lax.rem(me + d, 8)
            self.copies.append(
                pltpu.make_async_remote_copy(
                    src_ref=src(d, peer),
                    dst_ref=dst(d),
                    send_sem=s.ar_send.at[j, number, d],
                    recv_sem=s.ar_recv.at[j, number, d],
                    device_id=peer_id(peer),
                    device_id_type=MESH,
                )
            )

    def start(self):
        for copy in self.copies:
            copy.start()

    def finish(self):
        for copy in self.copies:
            copy.wait()


class Reduce:
    def __init__(self, s, j):
        lat, lon = lax.axis_index("lat"), lax.axis_index("lon")
        self.s, self.j = s, j
        self.line, self.z, self.lat = lax.rem(lon, 8), lon // 8, lat
        in_line = lambda p: (lat, (lon // 8) * 8 + p)
        in_z = lambda p: (lat, p * 8 + lax.rem(lon, 8))
        in_lat = lambda p: (p, lon)
        line, z = self.line, self.z
        self.stages = [
            Stage(s, j, 0, line, in_line, lambda d, p: s.send.at[j, p], lambda d: s.in1.at[j, d]),
            Stage(s, j, 1, z, in_z, lambda d, p: s.sum1.at[j, p], lambda d: s.in2.at[j, d]),
            Stage(s, j, 2, lat, in_lat, lambda d, p: s.sum2.at[j], lambda d: s.in3.at[j, d]),
            Stage(s, j, 3, z, in_z, lambda d, p: s.gather.at[j, z], lambda d: s.gather.at[j, z]),
            Stage(
                s, j, 4, line, in_line,
                lambda d, p: s.red.at[j, line], lambda d: s.red.at[j, line],
            ),
        ]

    def step(self, number):
        s, j = self.s, self.j
        if number > 0:
            self.stages[number - 1].finish()
        if number == 1:
            total = s.send[j, self.line].astype(F32)
            for d in range(1, 8):
                total = total + s.in1[j, d].astype(F32)
            for p in range(6):
                s.sum1[j, p] = total[32 * p : 32 * p + 32].astype(BF16)
            for p in range(6, 8):
                s.sum1[j, p] = jnp.zeros((32, 128), BF16)
        if number == 2:
            total = s.sum1[j, self.z].astype(F32)
            for d in range(1, 8):
                total = total + s.in2[j, d].astype(F32)
            s.sum2[j] = total.astype(BF16)
        if number == 3:
            own = s.sum2[j].astype(F32)
            total = own
            for d in range(1, 8):
                total = total + s.in3[j, d].astype(F32)
            rows = lax.broadcasted_iota(jnp.int32, (32, 1), 0) + self.z * 32
            table_until = jnp.where(self.line >= 6, 144, 0)
            s.gather[j, self.z] = jnp.where(rows < table_until, own, total).astype(BF16)
        if number == 4:
            for p in range(6):
                s.red[j, self.line, 32 * p : 32 * p + 32, :] = s.gather[j, p]
        if number < 5:
            self.stages[number].start()


def signal_partners():
    barrier = pltpu.get_barrier_semaphore()
    lat, lon = lax.axis_index("lat"), lax.axis_index("lon")
    nlat, nlon = lax.axis_size("lat"), lax.axis_size("lon")

    def signal(a, b):
        pl.semaphore_signal(barrier, inc=1, device_id=(a, b), device_id_type=MESH)

    for da, db in ((0, 1), (1, 0), (1, 1)):
        signal(lax.rem(lat + da, nlat), lax.rem(lon + db, nlon))
        signal(lax.rem(lat - da + nlat, nlat), lax.rem(lon - db + nlon, nlon))
    line, z = lax.rem(lon, 8), lon // 8
    for d in range(1, 8):
        signal(lat, z * 8 + lax.rem(line + d, 8))
        signal(lat, lax.rem(z + d, 8) * 8 + line)
        signal(lax.rem(lat + d, 8), lon)
    return barrier, 6 + 21


SCRATCH = dict(
    nat=pltpu.VMEM((144, 192), F32),
    tab=pltpu.VMEM((6, 24, 144), F32),
    wide=pltpu.VMEM((2, 144, 1024), F32),
    bias1=pltpu.VMEM((144, 864), F32),
    bias2=pltpu.VMEM((2, 72, 432), F32),
    ds=pltpu.VMEM((144, 1024), F32),
    normed=pltpu.VMEM((2, 144, 192), F32),
    inverse=pltpu.VMEM((2, 144, 1), F32),
    scaled=pltpu.VMEM((2, 144, 192), BF16),
    k=pltpu.VMEM((2, 144, 192), F32),
    v=pltpu.VMEM((2, 144, 192), F32),
    qm=pltpu.VMEM((2, 864, 192), BF16),
    probs=pltpu.VMEM((2, 144, 864), F32),
    mixed_t=pltpu.VMEM((2, 2, 192, 144), F32),
    grad=pltpu.VMEM((192, 768), F32),
    extra=pltpu.VMEM((192, 256), F32),
    halo_out=pltpu.VMEM((4, 4, 48, 192), BF16),
    halo_in=pltpu.VMEM((4, 4, 48, 192), BF16),
    send=pltpu.VMEM((2, 8, 192, 128), BF16),
    in1=pltpu.VMEM((2, 8, 192, 128), BF16),
    sum1=pltpu.VMEM((2, 8, 32, 128), BF16),
    in2=pltpu.VMEM((2, 8, 32, 128), BF16),
    sum2=pltpu.VMEM((2, 32, 128), BF16),
    in3=pltpu.VMEM((2, 8, 32, 128), BF16),
    gather=pltpu.VMEM((2, 8, 32, 128), BF16),
    red=pltpu.VMEM((2, 8, 192, 128), BF16),
    halo_send=pltpu.SemaphoreType.DMA((4, 3)),
    halo_recv=pltpu.SemaphoreType.DMA((4, 3)),
    ar_send=pltpu.SemaphoreType.DMA((2, 5, 8)),
    ar_recv=pltpu.SemaphoreType.DMA((2, 5, 8)),
)


class Names:
    pass


def main_kernel(
    x_ref, cot_ref, gains_ref, wqkv_ref, wproj_ref, tab_ref, pad_ref,
    perm_ref, to_ref, from_ref, exp1_ref, exp2_ref, one1_ref, one2_ref, info_ref,
    out_ref, dx_ref, red_ref, *scratch,
):
    s = Names()
    for name, ref in zip(SCRATCH, scratch):
        setattr(s, name, ref)
    lat = lax.axis_index("lat")
    barrier, expected = signal_partners()

    s.tab[...] = jnp.zeros((6, 24, 144), F32)
    s.ds[:, 768:1024] = jnp.zeros((144, 256), F32)
    s.extra[...] = jnp.zeros((192, 256), F32)

    def load(ref):
        for l in range(2):
            for r in range(6):
                at = 72 * l + 12 * r
                s.nat[at : at + 12, :] = ref[l, r].astype(F32)
        return s.nat[...].astype(BF16)

    def save(ref, value):
        s.nat[...] = value
        for l in range(2):
            for r in range(6):
                at = 72 * l + 12 * r
                ref[l, r] = s.nat[at : at + 12, :].astype(BF16)

    gain1, gain2 = gains_ref[0:1, :], gains_ref[1:2, :]
    x1 = nn(perm_ref[0], load(x_ref))
    expand_first(s, tab_ref, exp1_ref, info_ref, pad_ref, lat)
    first = forward(s, 0, x1, gain1, wqkv_ref, wproj_ref, lambda g: s.bias1[...], 1)
    pl.semaphore_wait(barrier, expected)

    h_first, h_cot, h_out, h_grad = [Halo(s, i, i < 2) for i in range(4)]
    h_first.start(nn(to_ref[1], first).astype(BF16))
    h_cot.start(nn(to_ref[0], load(cot_ref)).astype(BF16))
    expand_second(s, tab_ref, exp2_ref, info_ref, pad_ref, lat)
    x2 = nn(from_ref[2], h_first.finish())
    second = forward(s, 1, x2, gain2, wqkv_ref, wproj_ref, lambda g: s.bias2[g], 2)
    h_out.start(nn(to_ref[2], second).astype(BF16))
    g2 = nn(from_ref[2], h_cot.finish()).astype(BF16)
    dh2, saved2 = backward(s, 1, g2, gain2, wqkv_ref, wproj_ref, 2)
    h_grad.start(nn(to_ref[2], dh2).astype(BF16))
    gradients(s, 1, g2, saved2, fold_second(s, one2_ref, info_ref), 2)
    reduce2, reduce1 = Reduce(s, 1), Reduce(s, 0)
    reduce2.step(0)
    save(out_ref, nn(from_ref[0], h_out.finish()))
    g1 = nn(from_ref[1], h_grad.finish()).astype(BF16)
    reduce2.step(1)
    dx, saved1 = backward(s, 0, g1, gain1, wqkv_ref, wproj_ref, 1)
    reduce2.step(2)
    gradients(s, 0, g1, saved1, fold_first(s, one1_ref, info_ref), 1)
    reduce1.step(0)
    reduce2.step(3)
    save(dx_ref, nn(perm_ref[1], dx))
    reduce2.step(4)
    for number in range(1, 6):
        reduce1.step(number)
    reduce2.step(5)
    red_ref[...] = s.red[...]


def finish_kernel(red_ref, o_ref, d_ref, out_ref, dx_ref, gains_ref, dqkv_ref, dproj_ref, dtab_ref):
    out_ref[...] = o_ref[...]
    dx_ref[...] = d_ref[...]
    for j in range(2):
        for c in range(4):
            dqkv_ref[j, :, 128 * c : 128 * c + 128] = red_ref[j, c].astype(F32)
        mid = red_ref[j, 4].astype(F32)
        dqkv_ref[j, :, 512:576] = mid[:, 0:64]
        dproj_ref[j, :, 0:64] = mid[:, 64:128]
        dproj_ref[j, :, 64:192] = red_ref[j, 5].astype(F32)
        left = red_ref[j, 6].astype(F32)
        right = red_ref[j, 7].astype(F32)
        for h in range(HEADS):
            dtab_ref[j, 0, h, :, 0:128] = left[24 * h : 24 * h + 23]
            dtab_ref[j, 0, h, :, 128:144] = right[24 * h : 24 * h + 23, 0:16]
        gains_ref[j : j + 1, 0:128] = left[144:145]
        gains_ref[j : j + 1, 128:192] = right[144:145, 0:64]


def body(inputs, cotangent, gains, qkv_weights, proj_weights, bias_tables, pad_rows):
    vmem = pl.BlockSpec(memory_space=pltpu.VMEM)
    smem = pl.BlockSpec(memory_space=pltpu.SMEM)
    field = jax.ShapeDtypeStruct((2, 6, 12, 192), BF16)
    out, dx, red = pl.pallas_call(
        main_kernel,
        out_shape=(field, field, jax.ShapeDtypeStruct((2, 8, 192, 128), BF16)),
        in_specs=[vmem] * 6 + [smem] + [vmem] * 8,
        out_specs=(vmem,) * 3,
        scratch_shapes=list(SCRATCH.values()),
        compiler_params=pltpu.CompilerParams(
            collective_id=0, has_side_effects=True, vmem_limit_bytes=48 * 2**20
        ),
        name="both_blocks",
    )(inputs, cotangent, gains, qkv_weights, proj_weights, bias_tables, pad_rows, *constants())
    return pl.pallas_call(
        finish_kernel,
        out_shape=(
            field,
            field,
            jax.ShapeDtypeStruct((2, 192), F32),
            jax.ShapeDtypeStruct((2, 192, 576), F32),
            jax.ShapeDtypeStruct((2, 192, 192), F32),
            jax.ShapeDtypeStruct((2, 1, 6, 23, 144), F32),
        ),
        in_specs=[vmem] * 3,
        out_specs=(vmem,) * 6,
        compiler_params=pltpu.CompilerParams(vmem_limit_bytes=32 * 2**20),
        name="unpack",
    )(red, out, dx)


def solution(mesh):
    field = P(None, "lat", "lon", None)
    tables = P(None, "lat", None, None, None)
    return jax.shard_map(
        body,
        mesh=mesh,
        in_specs=(field, field, P(), P(), P(), tables, P()),
        out_specs=(field, field, P(), P(), P(), tables),
        check_vma=False,
    )
```

time: 1500 us -> 117 us (0.08)
  waiting for transfers between devices: 1150 us -> 0 us
  blocking collectives: 107 us -> 0 us
  Pallas kernels: 0 us -> 103 us
  local copies, waits for them, and re-layouts: 85.6 us -> 13 us
  matrix products: 64.1 us -> 0 us
  starting transfers between devices: 51.6 us -> 0 us
  other arithmetic: 22.8 us -> 0 us
    psum x2 -> x0, waiting for transfers between devices: 1150 us -> none  [the longest x1 673 us: body(): table_total = lax.psum(stacked[3], 'lon')]
    psum x1 -> x0, blocking collectives: 107 us -> none  [body(): lax.psum((stacked[0], stacked[1], stacked[2]), ('lat', 'lon'))]
    pallas_call x0 -> x2, Pallas kernels: none -> 103 us  [the longest x1 101 us: body(): pl.pallas_call(main_kernel, out_shape=(field, field, jax.ShapeDtypeStruct...]
    another operation x18 -> x0, local copies, waits for them, and re-layouts: 68.2 us -> none
    dot_general x28 -> x0, matrix products: 64.1 us -> none  [the longest x24 24.8 us: product(): return jnp.einsum(form, left, right, preferred_element_type=jnp.float32)]
    ppermute x8 -> x0, starting transfers between devices: 51.5 us -> none  [shifted(): lax.ppermute(value, axis, [(i, (i + by) % devices) for i in range(devices)])]
  transfers between devices with their start and end apart: 10 -> 0, of which waited for: 4 -> 0; matrix products, arithmetic and copies ran while one was open for 5% -> 0% of each run, Pallas kernels for 0% -> 0%
where the time goes in v1:
time: 117 us; the launch traced here: 116 us
  Pallas kernels  103 us (88%)
  local copies, waits for them, and re-layouts  13 us (11%)
    pallas_call x1, Pallas kernels, body(): pl.pallas_call(main_kernel, out_shape=(field, field, jax.ShapeDtypeStruct...  101 us
    unnamed x27, local copies, waits for them, and re-layouts  10.5 us
    pallas_call x3, local copies, waits for them, and re-layouts, body(): pl.pallas_call(finish_kernel, out_shape=(field, field, jax.ShapeDtypeStru...  2.42 us

profile of v1, /device:TPU:1, one launch (start us, length us, event | category | flops | bytes accessed | tf_op | source)
XLA Modules:
  0.0 116.3 jit_solution(13652070973965688894)
XLA Ops:
  0.6 0.0 copy-start
  0.6 1.0 copy.21.x_ref
  1.6 0.9 copy.22.cot_ref
  2.5 0.0 copy-start.9
  2.5 0.0 copy-start.10
  2.6 0.0 copy-start.11
  2.6 1.0 copy.23.tab_ref
  3.6 0.0 copy-done
  3.6 0.0 copy-done.9
  3.6 0.0 copy-done.10
  3.6 0.0 copy-done.11
  3.6 0.0 copy-start.1
  3.6 1.0 copy-done.1
  4.6 0.0 copy-start.2
  4.6 1.0 copy-done.2
  5.7 0.0 copy-start.3
  5.7 1.0 copy-done.3
  6.6 0.0 copy-start.4
  6.6 1.0 copy-done.4
  7.6 0.0 copy-start.5
  7.6 0.9 copy-done.5
  8.5 0.0 copy-start.6
  8.5 0.9 copy-done.6
  9.4 0.0 copy-start.7
  9.4 0.9 copy-done.7
  10.4 0.0 copy-start.8
  10.4 0.9 copy-done.8
  11.3 101.4 %both_blocks.1 = (bf16[2,6,12,192]{3,2,1,0:T(8,128)(2,1)S(1)}, bf16[2,6,12,192]{3,2,1,0:T(8,128)(2,1)S(1)}, bf16[2,8,192,128]{3,2,1,0:T(8,128)(2,1)S(1)}) custom-call(bf16[2,6,12,192]{3,2,1,0:T(8,128)(2,1)S(1)} %copy.21.x_ref, bf16[2,6,12,192]{3,2,1,0:T(8,128)(2,1)S(1)} %copy.22.cot_ref, f32[2,192]{1,0:T(2,128)S(1)} %copy-done.10, ...), custom_call_target="tpu_custom_call" | custom-call | tf_op jit(solution)/shard_map/both_blocks/pallas_call | solution.py:557
  112.7 1.2 unpack.1
  113.8 0.7 copy.24
  114.5 0.7 copy.25
  115.3 1.0 copy.26
Async XLA Ops:
  0.6 2.9 %copy-start = (bf16[2,216,1024]{2,1,0:T(8,128)(2,1)S(1)}, bf16[2,216,1024]{2,1,0:T(8,128)(2,1)}, u32[]{:S(2)}) copy-start(bf16[2,216,1024]{2,1,0:T(8,128)(2,1)} %constant.19.clone.exp1_ref) | copy-start | bytes 2654212
  2.5 1.0 copy-start.9
  2.5 1.0 copy-start.10
  2.6 1.0 copy-start.11
  3.6 1.0 copy-start.1
  4.6 1.0 copy-start.2
  5.7 1.0 copy-start.3
  6.6 1.0 copy-start.4
  7.6 0.9 copy-start.5
  8.5 0.9 copy-start.6
  9.4 0.9 copy-start.7
  10.4 0.9 copy-start.8

commit v2 on v1

v2 whole, which is shorter than its diff:
```python
import jax
import jax.numpy as jnp
from jax import lax
from jax.experimental import pallas as pl
from jax.experimental.pallas import tpu as pltpu
from jax.sharding import PartitionSpec as P

F32 = jnp.float32
BF16 = jnp.bfloat16
MESH = pl.DeviceIdType.MESH
HEADS = 6
SCALE = 32 ** (-0.5)


def div(x, d):
    return (x * (-(-(2**20) // d))) >> 20


def tokens_of(order, n):
    i = lax.broadcasted_iota(jnp.int32, (n, 1), 0)
    used = i < n
    if order == "n":
        r = div(i, 24)
        c = div(i - 24 * r, 2)
        l = i - 24 * r - 2 * c
    elif order == "a":
        c = div(i, 12)
        l = div(i - 12 * c, 6)
        r = i - 12 * c - 6 * l
    elif order == "b":
        l = div(i, 72)
        c = div(i - 72 * l, 6)
        r = i - 72 * l - 6 * c
    else:
        q = div(i, 48)
        inner = i - 48 * q
        used = inner < 36
        l = div(inner, 18)
        r = div(inner - 18 * l, 6)
        c = inner - 18 * l - 6 * r
        r, c = r + 3 * (q >> 1), c + 6 * (q & 1)
    return l, r, c, used


def place_in(order, l, r, c):
    if order == "n":
        return 24 * r + 2 * c + l
    if order == "a":
        return 12 * c + 6 * l + r
    if order == "b":
        return 72 * l + 6 * c + r
    lower, right = (r >= 3).astype(jnp.int32), (c >= 6).astype(jnp.int32)
    return 48 * (2 * lower + right) + 18 * l + 6 * (r - 3 * lower) + c - 6 * right


def reorder(to, of):
    size = {"s": 192}
    n, m = size.get(to, 144), size.get(of, 144)
    l, r, c, used = tokens_of(to, n)
    place = jnp.where(used, place_in(of, l, r, c), -1)
    return jnp.where(place == lax.broadcasted_iota(jnp.int32, (n, m), 1), 1.0, 0.0).astype(BF16)


def spread(lanes, step, par, parts):
    i = lax.broadcasted_iota(jnp.int32, (72 * parts, 1), 0)
    part = div(i, 72)
    h = div(i - 72 * part, 24)
    o = i - 72 * part - 24 * h
    start = 12 * step * par + 24 * step * h + (22 - o) * step
    at = lax.broadcasted_iota(jnp.int32, (72 * parts, lanes), 1) - start
    return jnp.where((at >= 0) & (at < step), 1.0, 0.0).astype(BF16)


def lane_info(lanes, step):
    lane = lax.broadcasted_iota(jnp.int32, (1, lanes), 1)
    head = div(lane, 12 * step)
    parity = jnp.where(head < HEADS, head & 1, 2)
    return lane - step * div(lane, step), lane - 12 * step * head, parity


def nn(a, b):
    return lax.dot_general(a, b, (((1,), (0,)), ((), ())), preferred_element_type=F32)


def nt(a, b):
    return lax.dot_general(a, b, (((1,), (1,)), ((), ())), preferred_element_type=F32)


def tn(a, b):
    return lax.dot_general(a, b, (((0,), (0,)), ((), ())), preferred_element_type=F32)


def head_stack(x):
    lane = lax.broadcasted_iota(jnp.int32, (1, 192), 1)
    parts = [jnp.where((lane >= 32 * h) & (lane < 32 * h + 32), x, 0.0) for h in range(HEADS)]
    return jnp.concatenate(parts, 0).astype(BF16)


def head_diagonal(x, n):
    return jnp.concatenate(
        [x[32 * h : 32 * h + 32, n * h : n * h + n] for h in range(HEADS)], 0
    )


def split_table(s, block):
    out = []
    for h in range(HEADS):
        s.tab[h, 0:23, :] = s.tab_in[block, h, :, 0, :]
    for par in range(2):
        parts = [[], [], []]
        for h in range(3):
            t = s.tab[2 * h + par]
            hi = t.astype(BF16).astype(F32)
            rest = t - hi
            mid = rest.astype(BF16).astype(F32)
            for part, value in zip(parts, (hi, mid, rest - mid)):
                part.append(value)
        out.append(jnp.concatenate(sum(parts, []), 0).astype(BF16))
    return out


def row_flags(s, start):
    rows = lax.broadcasted_iota(jnp.int32, (6, 1), 0)
    flags = jnp.zeros((6, 1), jnp.int32)
    for r in range(6):
        flags = jnp.where(rows == r, s.pad[lax.rem(start + r, 48)], flags)
    return rows, flags == 1


def expand_first(s, lat):
    for par, parts in enumerate(split_table(s, 0)):
        s.wide[par] = tn(parts, spread(1024, 12, par, 3))
    entry, token, parity = lane_info(1024, 12)
    token, odd = token[:, 0:864], parity[:, 0:864] == 1
    rows, valid = row_flags(s, 6 * lat)
    for lk in range(2):
        strips = []
        for par in range(2):
            strip = jnp.zeros((6, 1024), F32)
            for e in range(12):
                at = 72 * (e // 6) + 36 * lk + 6 * (e % 6)
                strip = jnp.where(entry == e, s.wide[par, at : at + 6, :], strip)
            strips.append(strip)
        for ck in range(12):
            turn = (1024 - (11 - ck) * 12) % 1024
            even_part, odd_part = [
                (pltpu.roll(x, turn, 1) if turn else x)[:, 0:864] for x in strips
            ]
            at = 12 * ck + 6 * lk
            keep = valid | (token == rows + at)
            s.bias1[at : at + 6, :] = jnp.where(
                keep, jnp.where(odd, odd_part, even_part), -1e30
            )


def expand_second(s, lat):
    for par, parts in enumerate(split_table(s, 1)):
        s.wide[par, :, 0:512] = tn(parts, spread(512, 6, par, 3))
    entry, token, parity = lane_info(512, 6)
    token, odd = token[:, 0:432], parity[:, 0:432] == 1
    rows, valid = row_flags(s, 6 * lat + 3)
    q_band = jnp.where(lat == 7, (entry[:, 0:432] >= 3).astype(jnp.int32), 0)
    k_band = jnp.where(lat == 7, (rows >= 3).astype(jnp.int32), 0)
    same = q_band == k_band
    for lev in range(2):
        strips = []
        for par in range(2):
            strip = jnp.zeros((6, 512), F32)
            for e in range(6):
                at = 108 * (1 - lev) + 6 * e
                strip = jnp.where(entry == e, s.wide[par, at : at + 6, 0:512], strip)
            strips.append(strip)
        for ck in range(12):
            turn = (512 - (11 - ck) * 6) % 512
            even_part, odd_part = [
                (pltpu.roll(x, turn, 1) if turn else x)[:, 0:432] for x in strips
            ]
            at = 6 * ck
            keep = (valid | (token == rows + at)) & same
            s.bias2[lev, at : at + 6, :] = jnp.where(
                keep, jnp.where(odd, odd_part, even_part), -1e30
            )


def fold_first(s):
    entry, _, parity = lane_info(1024, 12)
    for par in range(2):
        mine = parity == par
        for lk in range(2):
            acc = jnp.zeros((6, 1024), F32)
            for ck in range(12):
                at = 12 * ck + 6 * lk
                piece = jnp.where(mine, s.ds[at : at + 6, :], 0.0)
                turn = (11 - ck) * 12
                acc = acc + (pltpu.roll(piece, turn, 1) if turn else piece)
            for e in range(12):
                at = 72 * (e // 6) + 36 * lk + 6 * (e % 6)
                s.wide[par, at : at + 6, :] = jnp.where(entry == e, acc, 0.0)
    return [nt(spread(1024, 12, par, 1), s.wide[par].astype(BF16)) for par in range(2)]


def fold_second(s):
    entry, _, parity = lane_info(512, 6)
    s.wide[:, :, 0:512] = jnp.zeros((2, 144, 512), F32)
    for par in range(2):
        mine = parity == par
        for lev in range(2):
            acc = jnp.zeros((6, 512), F32)
            for ck in range(12):
                at = 72 * lev + 6 * ck
                piece = jnp.where(mine, s.ds[at : at + 6, 0:512], 0.0)
                turn = (11 - ck) * 6
                acc = acc + (pltpu.roll(piece, turn, 1) if turn else piece)
            for e in range(6):
                at = 108 * (1 - lev) + 6 * e
                s.wide[par, at : at + 6, 0:512] = jnp.where(entry == e, acc, 0.0)
    return [nt(spread(512, 6, par, 1), s.wide[par, :, 0:512].astype(BF16)) for par in range(2)]


def forward(s, j, x, gain, wqkv_ref, wproj_ref, bias, groups):
    n = 144 // groups
    center = x - jnp.mean(x, -1, keepdims=True)
    inverse = lax.rsqrt(jnp.mean(center * center, -1, keepdims=True) + 1e-05)
    normed = center * inverse
    scaled = (normed * gain).astype(BF16)
    packed = nn(scaled, wqkv_ref[j])
    q, k, v = packed[:, 0:192], packed[:, 192:384], packed[:, 384:576]
    s.normed[j] = normed
    s.inverse[j] = inverse
    s.scaled[j] = scaled
    s.k[j] = k
    s.v[j] = v
    attended = []
    for g in range(groups):
        rows = slice(g * n, g * n + n)
        qm = head_stack(q[rows])
        s.qm[j, g * 6 * n : (g + 1) * 6 * n, :] = qm
        scores = nt(k[rows].astype(BF16), qm) * SCALE + bias(g)
        weight = jnp.exp(scores - jnp.max(scores, 0, keepdims=True))
        probs = weight * (1.0 / jnp.sum(weight, 0, keepdims=True))
        s.probs[j, rows, 0 : 6 * n] = probs
        mixed_t = head_diagonal(tn(v[rows].astype(BF16), probs.astype(BF16)), n)
        s.mixed_t[j, g, :, 0:n] = mixed_t
        attended.append(tn(mixed_t.astype(BF16), wproj_ref[j]))
    att = attended[0] if groups == 1 else jnp.concatenate(attended, 0)
    return (x + att).astype(BF16)


def backward(s, j, g_in, gain, wqkv_ref, wproj_ref, groups):
    n = 144 // groups
    back = nt(g_in, wproj_ref[j])
    dqs, dks, dvs = [], [], []
    for g in range(groups):
        rows = slice(g * n, g * n + n)
        backm = head_stack(back[rows])
        probs = s.probs[j, rows, 0 : 6 * n]
        k = s.k[j, rows, :].astype(BF16)
        v = s.v[j, rows, :].astype(BF16)
        qm = s.qm[j, g * 6 * n : (g + 1) * 6 * n, :]
        d_probs = nt(v, backm)
        dvs.append(nn(probs.astype(BF16), backm))
        d_scores = probs * (d_probs - jnp.sum(d_probs * probs, 0, keepdims=True))
        s.ds[rows, 0 : 6 * n] = d_scores
        d_rounded = (d_scores * SCALE).astype(BF16)
        dks.append(nn(d_rounded, qm))
        dqs.append(head_diagonal(tn(k, d_rounded), n).T)
    if groups == 1:
        dq, dk, dv = dqs[0], dks[0], dvs[0]
    else:
        dq, dk, dv = [jnp.concatenate(p, 0) for p in (dqs, dks, dvs)]
    dq, dk, dv = dq.astype(BF16), dk.astype(BF16), dv.astype(BF16)
    w = wqkv_ref[j]
    d_scaled = nt(dq, w[:, 0:192]) + nt(dk, w[:, 192:384]) + nt(dv, w[:, 384:576])
    normed = s.normed[j]
    d_normed = d_scaled * gain
    d_hidden = s.inverse[j] * (
        d_normed
        - jnp.mean(d_normed, -1, keepdims=True)
        - normed * jnp.mean(d_normed * normed, -1, keepdims=True)
    )
    result = (g_in.astype(F32) + d_hidden).astype(BF16)
    return result, (dq, dk, dv, d_scaled)


def gradients(s, j, g_in, saved, folded, groups):
    n = 144 // groups
    dq, dk, dv, d_scaled = saved
    scaled = s.scaled[j]
    s.grad[:, 0:192] = tn(scaled, dq)
    s.grad[:, 192:384] = tn(scaled, dk)
    s.grad[:, 384:576] = tn(scaled, dv)
    d_proj = jnp.zeros((192, 192), F32)
    for g in range(groups):
        d_proj = d_proj + nn(
            s.mixed_t[j, g, :, 0:n].astype(BF16), g_in[g * n : g * n + n]
        )
    s.grad[:, 576:768] = d_proj
    for h in range(HEADS):
        s.extra[24 * h : 24 * h + 24, 0:144] = folded[h % 2][24 * (h // 2) : 24 * (h // 2) + 24]
    s.extra[144:145, 0:192] = jnp.sum(d_scaled * s.normed[j], 0, keepdims=True)
    for half in range(2):
        for slot in range(12):
            column, row = half * 384 + (slot // 4) * 128, (slot % 4) * 48
            s.payload[j, half, slot] = s.grad[row : row + 48, column : column + 128].astype(BF16)
        for slot, row in ((12, 144), (13, 0), (14, 48), (15, 96)):
            s.payload[j, half, slot] = s.extra[
                row : row + 48, 128 * half : 128 * half + 128
            ].astype(BF16)


class Halo:
    def __init__(self, s, which, forward_shift):
        lat, lon = lax.axis_index("lat"), lax.axis_index("lon")
        nlat, nlon = lax.axis_size("lat"), lax.axis_size("lon")
        self.s, self.which = s, which
        self.copies = []
        self.stay = 3 if forward_shift else 0
        for i, quarter in enumerate(q for q in range(4) if q != self.stay):
            if forward_shift:
                by_lat, by_lon = quarter // 2 - 1 + nlat, quarter % 2 - 1 + nlon
            else:
                by_lat, by_lon = quarter // 2, quarter % 2
            self.copies.append(
                pltpu.make_async_remote_copy(
                    src_ref=s.halo_out.at[which, quarter],
                    dst_ref=s.halo_in.at[which, 3 - quarter],
                    send_sem=s.halo_send.at[which, i],
                    recv_sem=s.halo_recv.at[which, i],
                    device_id=(lax.rem(lat + by_lat, nlat), lax.rem(lon + by_lon, nlon)),
                    device_id_type=MESH,
                )
            )

    def start(self, quarters):
        for q in range(4):
            self.s.halo_out[self.which, q] = quarters[48 * q : 48 * q + 48]
        for copy in self.copies:
            copy.start()
        stay = self.stay
        self.s.halo_in[self.which, 3 - stay] = quarters[48 * stay : 48 * stay + 48]

    def finish(self):
        for copy in self.copies:
            copy.wait()
        return jnp.concatenate([self.s.halo_in[self.which, q] for q in range(4)], 0)


def place():
    lat, lon = lax.axis_index("lat"), lax.axis_index("lon")
    line = lax.rem(lon, 8)
    return lat, lon, lat // 2, lax.rem(lat, 2), lon // 8, line // 2, lax.rem(line, 2)


def sibling():
    lat, lon, y, zh, zl, x, core = place()
    return lat, zl * 8 + x * 2 + 1 - core


def plane_peers():
    lat, lon, y, zh, zl, x, core = place()
    out = []
    for dy in range(4):
        for dx in range(4):
            if dx or dy:
                py, px = lax.rem(y + dy, 4), lax.rem(x + dx, 4)
                out.append((dx if dy == 0 else 0, (py * 2 + zh, zl * 8 + px * 2 + core), py * 4 + px))
    return out


def near_peers():
    lat, lon, y, zh, zl, x, core = place()
    quad = (zl // 4) * 4
    return [(lat, (quad + lax.rem(zl + d, 4)) * 8 + x * 2 + core) for d in range(1, 4)]


def far_peers():
    lat, lon, y, zh, zl, x, core = place()
    out = []
    for d in range(1, 4):
        z = lax.rem(zh * 8 + zl + 4 * d, 16)
        out.append((y * 2 + z // 8, lax.rem(z, 8) * 8 + x * 2 + core))
    return out


def half_peer():
    lat, lon, y, zh, zl, x, core = place()
    return lat, lax.rem(zl + 4, 8) * 8 + x * 2 + core


class Reduce:
    def __init__(self, s, j):
        lat, lon, y, zh, zl, x, core = place()
        self.s, self.j, self.core, self.x = s, j, core, x
        self.own = y * 4 + x
        self.near, self.far, self.half = lax.rem(zl, 4), zh * 2 + zl // 4, zl // 4
        self.used = 0
        own, table = self.own, 16 + x
        near, far, half = self.near, self.far, self.half
        stages = [[self.copy(s.payload.at[j, 1 - core], s.in_core.at[j], sibling())], [], [], [], []]
        for i, (dx, peer, slot) in enumerate(plane_peers()):
            stages[1].append(self.copy(s.half.at[j, slot], s.in_plane.at[j, i], peer))
            stages[4].append(self.copy(s.red.at[j, core, own], s.red.at[j, core, own], peer))
            if dx:
                px = lax.rem(x + dx, 4)
                stages[1].append(self.copy(s.half.at[j, 13 + px], s.in_plane.at[j, 14 + dx], peer))
                stages[4].append(
                    self.copy(s.red.at[j, core, table], s.red.at[j, core, table], peer)
                )
        for peer in near_peers():
            stages[2].append(self.copy(s.near.at[j, near], s.near.at[j, near], peer))
        for peer in far_peers():
            stages[3].append(self.copy(s.far.at[j, far], s.far.at[j, far], peer))
        stages[3].append(self.copy(s.far_tab.at[j, half], s.far_tab.at[j, half], half_peer()))
        stages.append([self.copy(s.red.at[j, core], s.red.at[j, core], sibling())])
        self.stages = stages

    def copy(self, src, dst, peer):
        number, self.used = self.used, self.used + 1
        return pltpu.make_async_remote_copy(
            src_ref=src,
            dst_ref=dst,
            send_sem=self.s.ar_send.at[self.j, number],
            recv_sem=self.s.ar_recv.at[self.j, number],
            device_id=peer,
            device_id_type=MESH,
        )

    def step(self, number):
        s, j, core = self.s, self.j, self.core
        if number > 0:
            for copy in self.stages[number - 1]:
                copy.wait()
        if number == 1:
            for slot in range(16):
                total = s.payload[j, core, slot].astype(F32) + s.in_core[j, slot].astype(F32)
                s.half[j, slot] = total.astype(BF16)
        if number == 2:
            total = s.half[j, self.own].astype(F32)
            for i in range(15):
                total = total + s.in_plane[j, i].astype(F32)
            table = s.half[j, 13 + self.x].astype(F32)
            for i in range(15, 18):
                table = table + s.in_plane[j, i].astype(F32)
            s.near[j, self.near, 0:48] = total.astype(BF16)
            s.near[j, self.near, 48:96] = table.astype(BF16)
        if number == 3:
            total = s.near[j, 0].astype(F32)
            for i in range(1, 4):
                total = total + s.near[j, i].astype(F32)
            s.far[j, self.far] = total[0:48].astype(BF16)
            s.far_tab[j, self.half] = total[48:96].astype(BF16)
        if number == 4:
            total = s.far[j, 0].astype(F32)
            for i in range(1, 4):
                total = total + s.far[j, i].astype(F32)
            s.red[j, core, self.own] = total.astype(BF16)
            table = s.far_tab[j, 0].astype(F32) + s.far_tab[j, 1].astype(F32)
            s.red[j, core, 16 + self.x] = table.astype(BF16)
        if number < 6:
            for copy in self.stages[number]:
                copy.start()


def signal_partners():
    barrier = pltpu.get_barrier_semaphore()
    lat, lon = lax.axis_index("lat"), lax.axis_index("lon")
    nlat, nlon = lax.axis_size("lat"), lax.axis_size("lon")
    partners = [sibling()] + near_peers() + far_peers() + [p for _, p, _ in plane_peers()]
    partners.append(half_peer())
    for da, db in ((0, 1), (1, 0), (1, 1)):
        partners.append((lax.rem(lat + da, nlat), lax.rem(lon + db, nlon)))
        partners.append((lax.rem(lat - da + nlat, nlat), lax.rem(lon - db + nlon, nlon)))
    for partner in partners:
        pl.semaphore_signal(barrier, inc=1, device_id=partner, device_id_type=MESH)
    return barrier, len(partners)


SCRATCH = dict(
    x_in=pltpu.VMEM((6, 12, 2, 192), BF16),
    cot_in=pltpu.VMEM((6, 12, 2, 192), BF16),
    gains=pltpu.VMEM((2, 192), F32),
    wqkv=pltpu.VMEM((2, 192, 576), BF16),
    wproj=pltpu.VMEM((2, 192, 192), BF16),
    tab_in=pltpu.VMEM((2, 6, 23, 1, 144), F32),
    pad=pltpu.SMEM((48,), jnp.int32),
    loads=pltpu.SemaphoreType.DMA((7,)),
    tab=pltpu.VMEM((6, 24, 144), F32),
    wide=pltpu.VMEM((2, 144, 1024), F32),
    bias1=pltpu.VMEM((144, 864), F32),
    bias2=pltpu.VMEM((2, 72, 432), F32),
    ds=pltpu.VMEM((144, 1024), F32),
    normed=pltpu.VMEM((2, 144, 192), F32),
    inverse=pltpu.VMEM((2, 144, 1), F32),
    scaled=pltpu.VMEM((2, 144, 192), BF16),
    k=pltpu.VMEM((2, 144, 192), F32),
    v=pltpu.VMEM((2, 144, 192), F32),
    qm=pltpu.VMEM((2, 864, 192), BF16),
    probs=pltpu.VMEM((2, 144, 864), F32),
    mixed_t=pltpu.VMEM((2, 2, 192, 144), F32),
    grad=pltpu.VMEM((192, 768), F32),
    extra=pltpu.VMEM((192, 256), F32),
    halo_out=pltpu.VMEM((4, 4, 48, 192), BF16),
    halo_in=pltpu.VMEM((4, 4, 48, 192), BF16),
    payload=pltpu.VMEM((2, 2, 16, 48, 128), BF16),
    in_core=pltpu.VMEM((2, 16, 48, 128), BF16),
    half=pltpu.VMEM((2, 17, 48, 128), BF16),
    in_plane=pltpu.VMEM((2, 18, 48, 128), BF16),
    near=pltpu.VMEM((2, 4, 96, 128), BF16),
    far=pltpu.VMEM((2, 4, 48, 128), BF16),
    far_tab=pltpu.VMEM((2, 2, 48, 128), BF16),
    red=pltpu.VMEM((2, 2, 20, 48, 128), BF16),
    halo_send=pltpu.SemaphoreType.DMA((4, 3)),
    halo_recv=pltpu.SemaphoreType.DMA((4, 3)),
    ar_send=pltpu.SemaphoreType.DMA((2, 45)),
    ar_recv=pltpu.SemaphoreType.DMA((2, 45)),
)


class Names:
    pass


def main_kernel(
    x_ref, cot_ref, gains_ref, wqkv_ref, wproj_ref, tab_ref, pad_ref,
    out_ref, dx_ref, red_ref, *scratch,
):
    s = Names()
    for name, ref in zip(SCRATCH, scratch):
        setattr(s, name, ref)
    lat = lax.axis_index("lat")
    sources = dict(
        x_in=x_ref, tab_in=tab_ref, pad=pad_ref, gains=gains_ref, wqkv=wqkv_ref,
        wproj=wproj_ref, cot_in=cot_ref,
    )
    loads = {
        name: pltpu.make_async_copy(ref, getattr(s, name), s.loads.at[i])
        for i, (name, ref) in enumerate(sources.items())
    }
    for load in loads.values():
        load.start()
    barrier, expected = signal_partners()

    s.tab[...] = jnp.zeros((6, 24, 144), F32)
    s.ds[:, 768:1024] = jnp.zeros((144, 256), F32)
    s.extra[...] = jnp.zeros((192, 256), F32)
    s.half[:, 16] = jnp.zeros((2, 48, 128), BF16)
    s.red[:, :, 19] = jnp.zeros((2, 2, 48, 128), BF16)

    def field(ref):
        return ref[...].astype(F32).reshape(144, 192).astype(BF16)

    for name in ("tab_in", "pad"):
        loads[name].wait()
    expand_first(s, lat)
    for name in ("x_in", "gains", "wqkv", "wproj", "cot_in"):
        loads[name].wait()
    gain1, gain2 = s.gains[0:1, :], s.gains[1:2, :]
    x1 = nn(reorder("a", "n"), field(s.x_in))
    first = forward(s, 0, x1, gain1, s.wqkv, s.wproj, lambda g: s.bias1[...], 1)
    pl.semaphore_wait(barrier, expected)

    h_first, h_cot, h_out, h_grad = [Halo(s, i, i < 2) for i in range(4)]
    h_first.start(nn(reorder("s", "a"), first).astype(BF16))
    h_cot.start(nn(reorder("s", "n"), field(s.cot_in)).astype(BF16))
    expand_second(s, lat)
    x2 = nn(reorder("b", "s"), h_first.finish())
    second = forward(s, 1, x2, gain2, s.wqkv, s.wproj, lambda g: s.bias2[g], 2)
    h_out.start(nn(reorder("s", "b"), second).astype(BF16))
    g2 = nn(reorder("b", "s"), h_cot.finish()).astype(BF16)
    dh2, saved2 = backward(s, 1, g2, gain2, s.wqkv, s.wproj, 2)
    h_grad.start(nn(reorder("s", "b"), dh2).astype(BF16))
    gradients(s, 1, g2, saved2, fold_second(s), 2)
    reduce2, reduce1 = Reduce(s, 1), Reduce(s, 0)
    reduce2.step(0)
    out_ref[...] = nn(reorder("n", "s"), h_out.finish()).reshape(6, 12, 2, 192).astype(BF16)
    reduce2.step(1)
    g1 = nn(reorder("a", "s"), h_grad.finish()).astype(BF16)
    dx, saved1 = backward(s, 0, g1, gain1, s.wqkv, s.wproj, 1)
    reduce2.step(2)
    gradients(s, 0, g1, saved1, fold_first(s), 1)
    reduce1.step(0)
    dx_ref[...] = nn(reorder("n", "a"), dx).reshape(6, 12, 2, 192).astype(BF16)
    reduce1.step(1)
    reduce2.step(3)
    reduce1.step(2)
    reduce2.step(4)
    reduce1.step(3)
    reduce2.step(5)
    reduce1.step(4)
    reduce2.step(6)
    red_ref[1] = s.red[1]
    reduce1.step(5)
    reduce1.step(6)
    red_ref[0] = s.red[0]


def finish_kernel(red_ref, o_ref, d_ref, out_ref, dx_ref, gains_ref, dqkv_ref, dproj_ref, dtab_ref):
    out_ref[...] = o_ref[...]
    dx_ref[...] = d_ref[...]
    for j in range(2):
        for half in range(2):
            for slot in range(12):
                column, row = half * 3 + slot // 4, (slot % 4) * 48
                rows = slice(row, row + 48)
                value = red_ref[j, half, slot].astype(F32)
                if column < 4:
                    dqkv_ref[j, rows, 128 * column : 128 * column + 128] = value
                elif column == 4:
                    dqkv_ref[j, rows, 512:576] = value[:, 0:64]
                    dproj_ref[j, rows, 0:64] = value[:, 64:128]
                else:
                    dproj_ref[j, rows, 64:192] = value
            width = 128 if half == 0 else 16
            lanes = slice(128 * half, 128 * half + width)
            for third in range(3):
                value = red_ref[j, half, 16 + third].astype(F32)
                for i in range(2):
                    dtab_ref[j, 2 * third + i, :, 0, lanes] = value[24 * i : 24 * i + 23, 0:width]
        gains_ref[j : j + 1, 0:128] = red_ref[j, 0, 12].astype(F32)[0:1]
        gains_ref[j : j + 1, 128:192] = red_ref[j, 1, 12].astype(F32)[0:1, 0:64]


def body(inputs, cotangent, gains, qkv_weights, proj_weights, bias_tables, pad_rows):
    vmem = pl.BlockSpec(memory_space=pltpu.VMEM)
    hbm = pl.BlockSpec(memory_space=pltpu.HBM)
    field = jax.ShapeDtypeStruct((6, 12, 2, 192), BF16)
    out, dx, red = pl.pallas_call(
        main_kernel,
        out_shape=(field, field, jax.ShapeDtypeStruct((2, 2, 20, 48, 128), BF16)),
        in_specs=[hbm] * 7,
        out_specs=(vmem,) * 3,
        scratch_shapes=list(SCRATCH.values()),
        compiler_params=pltpu.CompilerParams(
            collective_id=0, has_side_effects=True, vmem_limit_bytes=48 * 2**20
        ),
        name="both_blocks",
    )(
        inputs.transpose(1, 2, 0, 3),
        cotangent.transpose(1, 2, 0, 3),
        gains,
        qkv_weights,
        proj_weights,
        bias_tables.transpose(0, 2, 3, 1, 4),
        pad_rows,
    )
    out, dx, d_gains, d_qkv, d_proj, d_tables = pl.pallas_call(
        finish_kernel,
        out_shape=(
            field,
            field,
            jax.ShapeDtypeStruct((2, 192), F32),
            jax.ShapeDtypeStruct((2, 192, 576), F32),
            jax.ShapeDtypeStruct((2, 192, 192), F32),
            jax.ShapeDtypeStruct((2, 6, 23, 1, 144), F32),
        ),
        in_specs=[vmem] * 3,
        out_specs=(vmem,) * 6,
        compiler_params=pltpu.CompilerParams(vmem_limit_bytes=32 * 2**20),
        name="unpack",
    )(red, out, dx)
    return (
        out.transpose(2, 0, 1, 3),
        dx.transpose(2, 0, 1, 3),
        d_gains,
        d_qkv,
        d_proj,
        d_tables.transpose(0, 3, 1, 2, 4),
    )


def solution(mesh):
    field = P(None, "lat", "lon", None)
    tables = P(None, "lat", None, None, None)
    return jax.shard_map(
        body,
        mesh=mesh,
        in_specs=(field, field, P(), P(), P(), tables, P()),
        out_specs=(field, field, P(), P(), P(), tables),
        check_vma=False,
    )
```

time: 117 us -> 90.8 us (0.78)
  Pallas kernels: 103 us -> 84.5 us
  local copies, waits for them, and re-layouts: 13 us -> 5.35 us
    pallas_call x1, Pallas kernels: 101 us -> 83.1 us  [body(): pl.pallas_call(main_kernel, out_shape=(field, field, jax.ShapeDtypeStruct...]
    unnamed x27 -> x14, local copies, waits for them, and re-layouts: 10.5 us -> 5.35 us
    pallas_call x3 -> x0, local copies, waits for them, and re-layouts: 2.42 us -> none  [body(): pl.pallas_call(finish_kernel, out_shape=(field, field, jax.ShapeDtypeStru...]
where the time goes in v2:
time: 90.8 us; the launch traced here: 90.5 us
  Pallas kernels  84.5 us (93%)
  local copies, waits for them, and re-layouts  5.35 us (6%)
    pallas_call x1, Pallas kernels, body(): pl.pallas_call(main_kernel, out_shape=(field, field, jax.ShapeDtypeStruct...  83.1 us
    unnamed x14, local copies, waits for them, and re-layouts  5.35 us

profile of v2, /device:TPU:1, one launch (start us, length us, event | category | flops | bytes accessed | tf_op | source)
XLA Modules:
  0.0 90.5 jit_solution(10786310404275274203)
XLA Ops:
  0.6 0.0 copy-start.5
  0.6 0.0 copy-start.6
  0.7 0.7 copy-done.5
  1.3 0.0 copy-done.6
  1.3 0.0 copy-start
  1.3 1.0 %copy-done = bf16[2,192,576]{2,1,0:T(8,128)(2,1)S(1)} copy-done((bf16[2,192,576]{2,1,0:T(8,128)(2,1)S(1)}, bf16[2,192,576]{2,1,0:T(8,128)(2,1)}, u32[]{:S(2)}) %copy-start) | copy-done | bytes 442392
  2.4 0.0 copy-start.1
  2.4 1.0 %copy-done.1 = f32[2,1,6,23,144]{4,1,3,2,0:T(1,128)S(1)} copy-done((f32[2,1,6,23,144]{4,1,3,2,0:T(1,128)S(1)}, f32[2,1,6,23,144]{4,1,3,2,0:T(1,128)}, u32[]{:S(2)}) %copy-start.1) | copy-done | bytes 159000
  3.3 0.0 copy-start.2
  3.3 0.9 %copy-done.2 = bf16[2,192,192]{2,1,0:T(8,128)(2,1)S(1)} copy-done((bf16[2,192,192]{2,1,0:T(8,128)(2,1)S(1)}, bf16[2,192,192]{2,1,0:T(8,128)(2,1)}, u32[]{:S(2)}) %copy-start.2) | copy-done | bytes 147480
  4.2 0.0 copy-start.3
  4.2 0.9 copy-done.3
  5.1 0.0 copy-start.4
  5.1 0.9 copy-done.4
  6.0 83.1 %both_blocks.1 = (bf16[6,12,2,192]{3,2,1,0:T(2,128)(2,1)S(1)}, bf16[6,12,2,192]{3,2,1,0:T(2,128)(2,1)S(1)}, bf16[2,2,20,48,128]{4,3,2,1,0:T(8,128)(2,1)S(1)}) custom-call(bf16[6,12,2,192]{3,2,1,0:T(2,128)(2,1)S(1)} %bitcast.7, bf16[6,12,2,192]{3,2,1,0:T(2,128)(2,1)S(1)} %bitcast.8, f32[2,192]{1,0:T(2,128)S(1)} %copy-done.5, ...), custom_call_target="tpu_custom_call" | custom-call | tf_op jit(solution)/shard_map/both_blocks/pallas_call | solution.py:627
  89.2 1.4 %unpack.1 = (bf16[6,12,2,192]{3,2,1,0:T(2,128)(2,1)}, bf16[6,12,2,192]{3,2,1,0:T(2,128)(2,1)}, f32[2,192]{1,0:T(2,128)}, f32[2,192,576]{2,1,0:T(8,128)}, f32[2,1...) custom-call(bf16[2,2,20,48,128]{4,3,2,1,0:T(8,128)(2,1)S(1)} %get-tuple-element.15.red_ref, ...), custom_call_target="tpu_custom_call" | custom-call | tf_op jit(solution)/shard_map/unpack/pallas_call | solution.py:646
Async XLA Ops:
  0.6 0.7 copy-start.5
  0.6 0.7 copy-start.6
  1.3 1.0 %copy-start = (bf16[2,192,576]{2,1,0:T(8,128)(2,1)S(1)}, bf16[2,192,576]{2,1,0:T(8,128)(2,1)}, u32[]{:S(2)}) copy-start(bf16[2,192,576]{2,1,0:T(8,128)(2,1)} %wqkv_ref.1) | copy-start | bytes 1327108
  2.4 1.0 %copy-start.1 = (f32[2,1,6,23,144]{4,1,3,2,0:T(1,128)S(1)}, f32[2,1,6,23,144]{4,1,3,2,0:T(1,128)}, u32[]{:S(2)}) copy-start(f32[2,1,6,23,144]{4,1,3,2,0:T(1,128)} %param.12) | copy-start | bytes 476932
  3.3 0.9 %copy-start.2 = (bf16[2,192,192]{2,1,0:T(8,128)(2,1)S(1)}, bf16[2,192,192]{2,1,0:T(8,128)(2,1)}, u32[]{:S(2)}) copy-start(bf16[2,192,192]{2,1,0:T(8,128)(2,1)} %wproj_ref.1) | copy-start | bytes 442372
  4.2 0.9 copy-start.3
  5.1 0.9 copy-start.4

commit v3 on v2

--- a/solution.py
+++ b/solution.py
@@ -9,6 +9,7 @@
 BF16 = jnp.bfloat16
 MESH = pl.DeviceIdType.MESH
 HEADS = 6
+VMEM_LIMIT = 62 * 2**20
 SCALE = 32 ** (-0.5)
 
 
@@ -32,9 +33,13 @@
         c = div(i - 72 * l, 6)
         r = i - 72 * l - 6 * c
     else:
-        q = div(i, 48)
-        inner = i - 48 * q
+        q = i >> 6
+        inner = i - 64 * q
         used = inner < 36
+        if order == "s1":
+            inner, used = inner - 36, (inner >= 36) & (inner < 54)
+        if order == "s2":
+            inner, used = inner - 18, (inner >= 36) & (inner < 54)
         l = div(inner, 18)
         r = div(inner - 18 * l, 6)
         c = inner - 18 * l - 6 * r
@@ -50,15 +55,32 @@
     if order == "b":
         return 72 * l + 6 * c + r
     lower, right = (r >= 3).astype(jnp.int32), (c >= 6).astype(jnp.int32)
-    return 48 * (2 * lower + right) + 18 * l + 6 * (r - 3 * lower) + c - 6 * right
+    quarter = 64 * (2 * lower + right)
+    inner = 18 * l + 6 * (r - 3 * lower) + c - 6 * right
+    if order == "s":
+        return quarter + inner
+    if order == "s1":
+        return jnp.where(inner < 18, quarter + 36 + inner, -1)
+    return jnp.where(inner >= 18, quarter + 18 + inner, -1)
 
 
 def reorder(to, of):
-    size = {"s": 192}
-    n, m = size.get(to, 144), size.get(of, 144)
+    n, m = [256 if order[0] == "s" else 144 for order in (to, of)]
     l, r, c, used = tokens_of(to, n)
     place = jnp.where(used, place_in(of, l, r, c), -1)
     return jnp.where(place == lax.broadcasted_iota(jnp.int32, (n, m), 1), 1.0, 0.0).astype(BF16)
+
+
+def pack(x, order):
+    wide, rest = x[:, 0:128], x[:, 128:192]
+    pairs = [nn(reorder(to, order), rest) for to in ("s1", "s2")]
+    return (nn(reorder("s", order), wide) + jnp.concatenate(pairs, 1)).astype(BF16)
+
+
+def unpack(x, order):
+    left, right = nn(reorder(order, "s1"), x), nn(reorder(order, "s2"), x)
+    rest = left[:, 0:64] + right[:, 64:128]
+    return jnp.concatenate([nn(reorder(order, "s"), x), rest], 1)
 
 
 def spread(lanes, step, par, parts):
@@ -333,16 +355,16 @@
 
     def start(self, quarters):
         for q in range(4):
-            self.s.halo_out[self.which, q] = quarters[48 * q : 48 * q + 48]
+            self.s.halo_out[self.which, q] = quarters[64 * q : 64 * q + 64]
         for copy in self.copies:
             copy.start()
         stay = self.stay
-        self.s.halo_in[self.which, 3 - stay] = quarters[48 * stay : 48 * stay + 48]
+        self.s.halo_in[self.which, 3 - stay] = quarters[64 * stay : 64 * stay + 64]
 
     def finish(self):
         for copy in self.copies:
             copy.wait()
-        return jnp.concatenate([self.s.halo_in[self.which, q] for q in range(4)], 0)
+        return self.s.halo_in[self.which].reshape(256, 128)
 
 
 def place():
@@ -484,6 +506,9 @@
     tab_in=pltpu.VMEM((2, 6, 23, 1, 144), F32),
     pad=pltpu.SMEM((48,), jnp.int32),
     loads=pltpu.SemaphoreType.DMA((7,)),
+    out=pltpu.VMEM((6, 12, 2, 192), BF16),
+    dx=pltpu.VMEM((6, 12, 2, 192), BF16),
+    stores=pltpu.SemaphoreType.DMA((4,)),
     tab=pltpu.VMEM((6, 24, 144), F32),
     wide=pltpu.VMEM((2, 144, 1024), F32),
     bias1=pltpu.VMEM((144, 864), F32),
@@ -499,8 +524,8 @@
     mixed_t=pltpu.VMEM((2, 2, 192, 144), F32),
     grad=pltpu.VMEM((192, 768), F32),
     extra=pltpu.VMEM((192, 256), F32),
-    halo_out=pltpu.VMEM((4, 4, 48, 192), BF16),
-    halo_in=pltpu.VMEM((4, 4, 48, 192), BF16),
+    halo_out=pltpu.VMEM((4, 4, 64, 128), BF16),
+    halo_in=pltpu.VMEM((4, 4, 64, 128), BF16),
     payload=pltpu.VMEM((2, 2, 16, 48, 128), BF16),
     in_core=pltpu.VMEM((2, 16, 48, 128), BF16),
     half=pltpu.VMEM((2, 17, 48, 128), BF16),
@@ -549,38 +574,46 @@
     def field(ref):
         return ref[...].astype(F32).reshape(144, 192).astype(BF16)
 
+    def store(number, value, ref):
+        copy = pltpu.make_async_copy(value, ref, s.stores.at[number])
+        copy.start()
+        return copy
+
     for name in ("tab_in", "pad"):
         loads[name].wait()
     expand_first(s, lat)
     for name in ("x_in", "gains", "wqkv", "wproj", "cot_in"):
         loads[name].wait()
     gain1, gain2 = s.gains[0:1, :], s.gains[1:2, :]
+    h_first, h_cot, h_out, h_grad = [Halo(s, i, i < 2) for i in range(4)]
+    reduce2, reduce1 = Reduce(s, 1), Reduce(s, 0)
+    cot = pack(field(s.cot_in), "n")
     x1 = nn(reorder("a", "n"), field(s.x_in))
+    pl.semaphore_wait(barrier, expected)
+    h_cot.start(cot)
+
     first = forward(s, 0, x1, gain1, s.wqkv, s.wproj, lambda g: s.bias1[...], 1)
-    pl.semaphore_wait(barrier, expected)
-
-    h_first, h_cot, h_out, h_grad = [Halo(s, i, i < 2) for i in range(4)]
-    h_first.start(nn(reorder("s", "a"), first).astype(BF16))
-    h_cot.start(nn(reorder("s", "n"), field(s.cot_in)).astype(BF16))
+    h_first.start(pack(first, "a"))
     expand_second(s, lat)
-    x2 = nn(reorder("b", "s"), h_first.finish())
+    x2 = unpack(h_first.finish(), "b")
     second = forward(s, 1, x2, gain2, s.wqkv, s.wproj, lambda g: s.bias2[g], 2)
-    h_out.start(nn(reorder("s", "b"), second).astype(BF16))
-    g2 = nn(reorder("b", "s"), h_cot.finish()).astype(BF16)
+    g2 = unpack(h_cot.finish(), "b").astype(BF16)
     dh2, saved2 = backward(s, 1, g2, gain2, s.wqkv, s.wproj, 2)
-    h_grad.start(nn(reorder("s", "b"), dh2).astype(BF16))
+    h_grad.start(pack(dh2, "b"))
+    h_out.start(pack(second, "b"))
     gradients(s, 1, g2, saved2, fold_second(s), 2)
-    reduce2, reduce1 = Reduce(s, 1), Reduce(s, 0)
     reduce2.step(0)
-    out_ref[...] = nn(reorder("n", "s"), h_out.finish()).reshape(6, 12, 2, 192).astype(BF16)
     reduce2.step(1)
-    g1 = nn(reorder("a", "s"), h_grad.finish()).astype(BF16)
+    g1 = unpack(h_grad.finish(), "a").astype(BF16)
     dx, saved1 = backward(s, 0, g1, gain1, s.wqkv, s.wproj, 1)
     reduce2.step(2)
     gradients(s, 0, g1, saved1, fold_first(s), 1)
     reduce1.step(0)
-    dx_ref[...] = nn(reorder("n", "a"), dx).reshape(6, 12, 2, 192).astype(BF16)
+    s.dx[...] = nn(reorder("n", "a"), dx).reshape(6, 12, 2, 192).astype(BF16)
+    stores = [store(0, s.dx, dx_ref)]
     reduce1.step(1)
+    s.out[...] = unpack(h_out.finish(), "n").reshape(6, 12, 2, 192).astype(BF16)
+    stores.append(store(1, s.out, out_ref))
     reduce2.step(3)
     reduce1.step(2)
     reduce2.step(4)
@@ -588,21 +621,32 @@
     reduce2.step(5)
     reduce1.step(4)
     reduce2.step(6)
-    red_ref[1] = s.red[1]
+    stores.append(store(2, s.red.at[1], red_ref.at[1]))
     reduce1.step(5)
     reduce1.step(6)
-    red_ref[0] = s.red[0]
-
-
-def finish_kernel(red_ref, o_ref, d_ref, out_ref, dx_ref, gains_ref, dqkv_ref, dproj_ref, dtab_ref):
-    out_ref[...] = o_ref[...]
-    dx_ref[...] = d_ref[...]
-    for j in range(2):
+    stores.append(store(3, s.red.at[0], red_ref.at[0]))
+    for copy in stores:
+        copy.wait()
+
+
+def finish_kernel(
+    red_ref, o_ref, d_ref, out_ref, dx_ref, gains_ref, dqkv_ref, dproj_ref, dtab_ref, red, sems
+):
+    copies = [
+        pltpu.make_async_copy(source, target, sems.at[i])
+        for i, (source, target) in enumerate(
+            ((red_ref.at[1], red.at[1]), (red_ref.at[0], red.at[0]), (o_ref, out_ref), (d_ref, dx_ref))
+        )
+    ]
+    for copy in copies:
+        copy.start()
+    for j in (1, 0):
+        copies[1 - j].wait()
         for half in range(2):
             for slot in range(12):
                 column, row = half * 3 + slot // 4, (slot % 4) * 48
                 rows = slice(row, row + 48)
-                value = red_ref[j, half, slot].astype(F32)
+                value = red[j, half, slot].astype(F32)
                 if column < 4:
                     dqkv_ref[j, rows, 128 * column : 128 * column + 128] = value
                 elif column == 4:
@@ -613,11 +657,13 @@
             width = 128 if half == 0 else 16
             lanes = slice(128 * half, 128 * half + width)
             for third in range(3):
-                value = red_ref[j, half, 16 + third].astype(F32)
+                value = red[j, half, 16 + third].astype(F32)
                 for i in range(2):
                     dtab_ref[j, 2 * third + i, :, 0, lanes] = value[24 * i : 24 * i + 23, 0:width]
-        gains_ref[j : j + 1, 0:128] = red_ref[j, 0, 12].astype(F32)[0:1]
-        gains_ref[j : j + 1, 128:192] = red_ref[j, 1, 12].astype(F32)[0:1, 0:64]
+        gains_ref[j : j + 1, 0:128] = red[j, 0, 12].astype(F32)[0:1]
+        gains_ref[j : j + 1, 128:192] = red[j, 1, 12].astype(F32)[0:1, 0:64]
+    for copy in copies[2:]:
+        copy.wait()
 
 
 def body(inputs, cotangent, gains, qkv_weights, proj_weights, bias_tables, pad_rows):
@@ -628,10 +674,10 @@
         main_kernel,
         out_shape=(field, field, jax.ShapeDtypeStruct((2, 2, 20, 48, 128), BF16)),
         in_specs=[hbm] * 7,
-        out_specs=(vmem,) * 3,
+        out_specs=(hbm,) * 3,
         scratch_shapes=list(SCRATCH.values()),
         compiler_params=pltpu.CompilerParams(
-            collective_id=0, has_side_effects=True, vmem_limit_bytes=48 * 2**20
+            collective_id=0, has_side_effects=True, vmem_limit_bytes=VMEM_LIMIT
         ),
         name="both_blocks",
     )(
@@ -653,9 +699,13 @@
             jax.ShapeDtypeStruct((2, 192, 192), F32),
             jax.ShapeDtypeStruct((2, 6, 23, 1, 144), F32),
         ),
-        in_specs=[vmem] * 3,
+        in_specs=[hbm] * 3,
         out_specs=(vmem,) * 6,
-        compiler_params=pltpu.CompilerParams(vmem_limit_bytes=32 * 2**20),
+        scratch_shapes=[
+            pltpu.VMEM((2, 2, 20, 48, 128), BF16),
+            pltpu.SemaphoreType.DMA((4,)),
+        ],
+        compiler_params=pltpu.CompilerParams(vmem_limit_bytes=VMEM_LIMIT),
         name="unpack",
     )(red, out, dx)
     return (

time: 90.8 us -> 80 us (0.88)
  local copies, waits for them, and re-layouts: 5.35 us -> 0 us
  Pallas kernels: 84.5 us -> 79.2 us
    pallas_call x1, Pallas kernels: 83.1 us -> 76.6 us  [body(): pl.pallas_call(main_kernel, out_shape=(field, field, jax.ShapeDtypeStruct...]
    unnamed x14 -> x0, local copies, waits for them, and re-layouts: 5.35 us -> none
    pallas_call x1, Pallas kernels: 1.35 us -> 2.66 us  [body(): pl.pallas_call(finish_kernel, out_shape=(field, field, jax.ShapeDtypeStru...]
where the time goes in v3:
time: 80 us; the launch traced here: 79.9 us
  Pallas kernels  79.2 us (99%)
    pallas_call x1, Pallas kernels, body(): pl.pallas_call(main_kernel, out_shape=(field, field, jax.ShapeDtypeStruct...  76.6 us
    pallas_call x1, Pallas kernels, body(): pl.pallas_call(finish_kernel, out_shape=(field, field, jax.ShapeDtypeStru...  2.66 us

profile of v3, /device:TPU:1, one launch (start us, length us, event | category | flops | bytes accessed | tf_op | source)
XLA Modules:
  0.0 79.9 jit_solution(3503834801069065810)
XLA Ops:
  0.6 76.6 %both_blocks.1 = (bf16[6,12,2,192]{3,2,1,0:T(2,128)(2,1)}, bf16[6,12,2,192]{3,2,1,0:T(2,128)(2,1)}, bf16[2,2,20,48,128]{4,3,2,1,0:T(8,128)(2,1)}) custom-call(bf16[6,12,2,192]{3,2,1,0:T(2,128)(2,1)} %bitcast.7, bf16[6,12,2,192]{3,2,1,0:T(2,128)(2,1)} %bitcast.8, f32[2,192]{1,0:T(2,128)} %gains_ref.1, bf16[2,192,576]{2,1,0:T(8,128)(2,1)} %wqkv_ref.1, ...), custom_call_target="tpu_custom_call" | custom-call | tf_op jit(solution)/shard_map/both_blocks/pallas_call | solution.py:673
  77.2 2.7 %unpack.1 = (bf16[6,12,2,192]{3,2,1,0:T(2,128)(2,1)}, bf16[6,12,2,192]{3,2,1,0:T(2,128)(2,1)}, f32[2,192]{1,0:T(2,128)}, f32[2,192,576]{2,1,0:T(8,128)}, f32[2,1...) custom-call(bf16[2,2,20,48,128]{4,3,2,1,0:T(8,128)(2,1)} %get-tuple-element.15.red_ref, ...), custom_call_target="tpu_custom_call" | custom-call | tf_op jit(solution)/shard_map/unpack/pallas_call | solution.py:692

commit v4 on v3

--- a/solution.py
+++ b/solution.py
@@ -124,14 +124,12 @@
     )
 
 
-def split_table(s, block):
+def split_table(tab):
     out = []
-    for h in range(HEADS):
-        s.tab[h, 0:23, :] = s.tab_in[block, h, :, 0, :]
     for par in range(2):
         parts = [[], [], []]
         for h in range(3):
-            t = s.tab[2 * h + par]
+            t = tab[2 * h + par]
             hi = t.astype(BF16).astype(F32)
             rest = t - hi
             mid = rest.astype(BF16).astype(F32)
@@ -150,7 +148,9 @@
 
 
 def expand_first(s, lat):
-    for par, parts in enumerate(split_table(s, 0)):
+    for h in range(HEADS):
+        s.tab[h, 0:23, :] = s.tab_in[0, h, :, 0, :]
+    for par, parts in enumerate(split_table(s.tab)):
         s.wide[par] = tn(parts, spread(1024, 12, par, 3))
     entry, token, parity = lane_info(1024, 12)
     token, odd = token[:, 0:864], parity[:, 0:864] == 1
@@ -176,8 +176,8 @@
 
 
 def expand_second(s, lat):
-    for par, parts in enumerate(split_table(s, 1)):
-        s.wide[par, :, 0:512] = tn(parts, spread(512, 6, par, 3))
+    for par, parts in enumerate(split_table(s.tab2)):
+        s.wide[par, 0:128, 0:512] = tn(parts, spread(512, 6, par, 3))
     entry, token, parity = lane_info(512, 6)
     token, odd = token[:, 0:432], parity[:, 0:432] == 1
     rows, valid = row_flags(s, 6 * lat + 3)
@@ -189,7 +189,7 @@
         for par in range(2):
             strip = jnp.zeros((6, 512), F32)
             for e in range(6):
-                at = 108 * (1 - lev) + 6 * e
+                at = 36 * (1 - lev) + 6 * e
                 strip = jnp.where(entry == e, s.wide[par, at : at + 6, 0:512], strip)
             strips.append(strip)
         for ck in range(12):
@@ -239,7 +239,7 @@
     return [nt(spread(512, 6, par, 1), s.wide[par, :, 0:512].astype(BF16)) for par in range(2)]
 
 
-def forward(s, j, x, gain, wqkv_ref, wproj_ref, bias, groups):
+def attend(s, j, x, gain, wqkv_ref, bias, groups):
     n = 144 // groups
     center = x - jnp.mean(x, -1, keepdims=True)
     inverse = lax.rsqrt(jnp.mean(center * center, -1, keepdims=True) + 1e-05)
@@ -252,7 +252,6 @@
     s.scaled[j] = scaled
     s.k[j] = k
     s.v[j] = v
-    attended = []
     for g in range(groups):
         rows = slice(g * n, g * n + n)
         qm = head_stack(q[rows])
@@ -261,20 +260,34 @@
         weight = jnp.exp(scores - jnp.max(scores, 0, keepdims=True))
         probs = weight * (1.0 / jnp.sum(weight, 0, keepdims=True))
         s.probs[j, rows, 0 : 6 * n] = probs
-        mixed_t = head_diagonal(tn(v[rows].astype(BF16), probs.astype(BF16)), n)
+
+
+def project(s, j, x, wproj_ref, groups):
+    n = 144 // groups
+    attended = []
+    for g in range(groups):
+        rows = slice(g * n, g * n + n)
+        v, probs = s.v[j, rows, :], s.probs[j, rows, 0 : 6 * n]
+        mixed_t = head_diagonal(tn(v.astype(BF16), probs.astype(BF16)), n)
         s.mixed_t[j, g, :, 0:n] = mixed_t
         attended.append(tn(mixed_t.astype(BF16), wproj_ref[j]))
     att = attended[0] if groups == 1 else jnp.concatenate(attended, 0)
     return (x + att).astype(BF16)
 
 
-def backward(s, j, g_in, gain, wqkv_ref, wproj_ref, groups):
+def head_backs(s, j, g_in, wproj_ref, groups):
     n = 144 // groups
     back = nt(g_in, wproj_ref[j])
+    for g in range(groups):
+        s.backm[j, g * 6 * n : (g + 1) * 6 * n, :] = head_stack(back[g * n : g * n + n])
+
+
+def backward(s, j, g_in, gain, wqkv_ref, groups):
+    n = 144 // groups
     dqs, dks, dvs = [], [], []
     for g in range(groups):
         rows = slice(g * n, g * n + n)
-        backm = head_stack(back[rows])
+        backm = s.backm[j, g * 6 * n : (g + 1) * 6 * n, :]
         probs = s.probs[j, rows, 0 : 6 * n]
         k = s.k[j, rows, :].astype(BF16)
         v = s.v[j, rows, :].astype(BF16)
@@ -333,33 +346,34 @@
 class Halo:
     def __init__(self, s, which, forward_shift):
         lat, lon = lax.axis_index("lat"), lax.axis_index("lon")
+        home_lat, home_lon = home()
         nlat, nlon = lax.axis_size("lat"), lax.axis_size("lon")
         self.s, self.which = s, which
-        self.copies = []
-        self.stay = 3 if forward_shift else 0
-        for i, quarter in enumerate(q for q in range(4) if q != self.stay):
+        self.copies, self.partners = [], []
+        for quarter in range(4):
+            down, right = quarter // 2, quarter % 2
             if forward_shift:
-                by_lat, by_lon = quarter // 2 - 1 + nlat, quarter % 2 - 1 + nlon
+                peer = runs_at(
+                    lax.rem(lat + down - 1 + nlat, nlat), lax.rem(lon + right - 1 + nlon, nlon)
+                )
             else:
-                by_lat, by_lon = quarter // 2, quarter % 2
+                peer = lax.rem(home_lat + down, nlat), lax.rem(home_lon + right, nlon)
+            self.partners.append(peer)
             self.copies.append(
                 pltpu.make_async_remote_copy(
                     src_ref=s.halo_out.at[which, quarter],
                     dst_ref=s.halo_in.at[which, 3 - quarter],
-                    send_sem=s.halo_send.at[which, i],
-                    recv_sem=s.halo_recv.at[which, i],
-                    device_id=(lax.rem(lat + by_lat, nlat), lax.rem(lon + by_lon, nlon)),
+                    send_sem=s.halo_send.at[which, quarter],
+                    recv_sem=s.halo_recv.at[which, quarter],
+                    device_id=peer,
                     device_id_type=MESH,
                 )
             )
 
     def start(self, quarters):
-        for q in range(4):
-            self.s.halo_out[self.which, q] = quarters[64 * q : 64 * q + 64]
+        self.s.halo_out[self.which] = quarters.reshape(4, 64, 128)
         for copy in self.copies:
             copy.start()
-        stay = self.stay
-        self.s.halo_in[self.which, 3 - stay] = quarters[64 * stay : 64 * stay + 64]
 
     def finish(self):
         for copy in self.copies:
@@ -367,10 +381,62 @@
         return self.s.halo_in[self.which].reshape(256, 128)
 
 
+class TableShare:
+    def __init__(self, s):
+        lat, lon, y, zh, zl, x, core = place()
+        self.s, self.core = s, core
+        self.leaves, self.arrives = zl >= 4, zl < 4
+        heads, others = pl.ds(3 * core, 3), pl.ds(3 - 3 * core, 3)
+        self.far = self.copy(s.tab2_own.at[heads], s.tab2.at[heads], far_peers()[0], 0)
+        self.pair = self.copy(s.tab2.at[heads], s.tab2.at[heads], sibling(), 1)
+
+    def copy(self, src, dst, peer, number):
+        return pltpu.make_async_remote_copy(
+            src_ref=src,
+            dst_ref=dst,
+            send_sem=self.s.tab_send.at[number],
+            recv_sem=self.s.tab_recv.at[number],
+            device_id=peer,
+            device_id_type=MESH,
+        )
+
+    def start(self):
+        @pl.when(self.leaves)
+        def _():
+            self.far.start()
+
+    def forward(self):
+        @pl.when(self.arrives)
+        def _():
+            self.far.wait_recv()
+            self.pair.start()
+
+    def finish(self):
+        @pl.when(self.leaves)
+        def _():
+            self.far.wait_send()
+            self.s.tab2[...] = self.s.tab2_own[...]
+
+        @pl.when(self.arrives)
+        def _():
+            self.pair.wait()
+
+
 def place():
     lat, lon = lax.axis_index("lat"), lax.axis_index("lon")
     line = lax.rem(lon, 8)
     return lat, lon, lat // 2, lax.rem(lat, 2), lon // 8, line // 2, lax.rem(line, 2)
+
+
+def runs_at(lat, lon):
+    z = lax.rem(lax.rem(lat, 2) * 8 + lon // 8 + 4, 16)
+    return (lat // 2) * 2 + z // 8, lax.rem(z, 8) * 8 + lax.rem(lon, 8)
+
+
+def home():
+    lat, lon, y, zh, zl, x, core = place()
+    z = lax.rem(zh * 8 + zl + 12, 16)
+    return y * 2 + z // 8, lax.rem(z, 8) * 8 + lax.rem(lon, 8)
 
 
 def sibling():
@@ -432,7 +498,13 @@
             stages[2].append(self.copy(s.near.at[j, near], s.near.at[j, near], peer))
         for peer in far_peers():
             stages[3].append(self.copy(s.far.at[j, far], s.far.at[j, far], peer))
-        stages[3].append(self.copy(s.far_tab.at[j, half], s.far_tab.at[j, half], half_peer()))
+        if j == 0:
+            stages[3].append(self.copy(s.far_tab.at[0, half], s.far_tab.at[0, half], half_peer()))
+        else:
+            for steps in (1, 2):
+                stages[3].append(
+                    self.copy(s.far_tab.at[1, 0], s.far_tab.at[1, steps], far_peers()[3 - steps])
+                )
         stages.append([self.copy(s.red.at[j, core], s.red.at[j, core], sibling())])
         self.stages = stages
 
@@ -470,28 +542,28 @@
             for i in range(1, 4):
                 total = total + s.near[j, i].astype(F32)
             s.far[j, self.far] = total[0:48].astype(BF16)
-            s.far_tab[j, self.half] = total[48:96].astype(BF16)
+            s.far_tab[j, self.half if j == 0 else 0] = total[48:96].astype(BF16)
         if number == 4:
             total = s.far[j, 0].astype(F32)
             for i in range(1, 4):
                 total = total + s.far[j, i].astype(F32)
             s.red[j, core, self.own] = total.astype(BF16)
-            table = s.far_tab[j, 0].astype(F32) + s.far_tab[j, 1].astype(F32)
+            if j == 0:
+                table = s.far_tab[0, 0].astype(F32) + s.far_tab[0, 1].astype(F32)
+            else:
+                own, one, two = [s.far_tab[1, i].astype(F32) for i in range(3)]
+                table = jnp.where(self.half == 1, own + one, one + two)
             s.red[j, core, 16 + self.x] = table.astype(BF16)
         if number < 6:
             for copy in self.stages[number]:
                 copy.start()
 
 
-def signal_partners():
+def signal_partners(halos):
     barrier = pltpu.get_barrier_semaphore()
-    lat, lon = lax.axis_index("lat"), lax.axis_index("lon")
-    nlat, nlon = lax.axis_size("lat"), lax.axis_size("lon")
-    partners = [sibling()] + near_peers() + far_peers() + [p for _, p, _ in plane_peers()]
-    partners.append(half_peer())
-    for da, db in ((0, 1), (1, 0), (1, 1)):
-        partners.append((lax.rem(lat + da, nlat), lax.rem(lon + db, nlon)))
-        partners.append((lax.rem(lat - da + nlat, nlat), lax.rem(lon - db + nlon, nlon)))
+    partners = halos[0].partners + halos[-1].partners
+    partners += far_peers() + near_peers() + [p for _, p, _ in plane_peers()]
+    partners += [sibling(), half_peer()]
     for partner in partners:
         pl.semaphore_signal(barrier, inc=1, device_id=partner, device_id_type=MESH)
     return barrier, len(partners)
@@ -510,6 +582,8 @@
     dx=pltpu.VMEM((6, 12, 2, 192), BF16),
     stores=pltpu.SemaphoreType.DMA((4,)),
     tab=pltpu.VMEM((6, 24, 144), F32),
+    tab2_own=pltpu.VMEM((6, 24, 128), F32),
+    tab2=pltpu.VMEM((6, 24, 128), F32),
     wide=pltpu.VMEM((2, 144, 1024), F32),
     bias1=pltpu.VMEM((144, 864), F32),
     bias2=pltpu.VMEM((2, 72, 432), F32),
@@ -520,6 +594,7 @@
     k=pltpu.VMEM((2, 144, 192), F32),
     v=pltpu.VMEM((2, 144, 192), F32),
     qm=pltpu.VMEM((2, 864, 192), BF16),
+    backm=pltpu.VMEM((2, 864, 192), BF16),
     probs=pltpu.VMEM((2, 144, 864), F32),
     mixed_t=pltpu.VMEM((2, 2, 192, 144), F32),
     grad=pltpu.VMEM((192, 768), F32),
@@ -532,12 +607,14 @@
     in_plane=pltpu.VMEM((2, 18, 48, 128), BF16),
     near=pltpu.VMEM((2, 4, 96, 128), BF16),
     far=pltpu.VMEM((2, 4, 48, 128), BF16),
-    far_tab=pltpu.VMEM((2, 2, 48, 128), BF16),
+    far_tab=pltpu.VMEM((2, 3, 48, 128), BF16),
     red=pltpu.VMEM((2, 2, 20, 48, 128), BF16),
-    halo_send=pltpu.SemaphoreType.DMA((4, 3)),
-    halo_recv=pltpu.SemaphoreType.DMA((4, 3)),
-    ar_send=pltpu.SemaphoreType.DMA((2, 45)),
-    ar_recv=pltpu.SemaphoreType.DMA((2, 45)),
+    halo_send=pltpu.SemaphoreType.DMA((4, 4)),
+    halo_recv=pltpu.SemaphoreType.DMA((4, 4)),
+    tab_send=pltpu.SemaphoreType.DMA((2,)),
+    tab_recv=pltpu.SemaphoreType.DMA((2,)),
+    ar_send=pltpu.SemaphoreType.DMA((2, 48)),
+    ar_recv=pltpu.SemaphoreType.DMA((2, 48)),
 )
 
 
@@ -563,9 +640,11 @@
     }
     for load in loads.values():
         load.start()
-    barrier, expected = signal_partners()
+    h_first, h_cot, h_out, h_grad = halos = [Halo(s, i, i < 2) for i in range(4)]
+    barrier, expected = signal_partners(halos)
 
     s.tab[...] = jnp.zeros((6, 24, 144), F32)
+    s.tab2_own[...] = jnp.zeros((6, 24, 128), F32)
     s.ds[:, 768:1024] = jnp.zeros((144, 256), F32)
     s.extra[...] = jnp.zeros((192, 256), F32)
     s.half[:, 16] = jnp.zeros((2, 48, 128), BF16)
@@ -581,31 +660,42 @@
 
     for name in ("tab_in", "pad"):
         loads[name].wait()
+    for h in range(HEADS):
+        for lev in range(2):
+            s.tab2_own[h, 0:23, 36 * lev : 36 * lev + 36] = s.tab_in[
+                1, h, :, 0, 108 * lev : 108 * lev + 36
+            ]
     expand_first(s, lat)
     for name in ("x_in", "gains", "wqkv", "wproj", "cot_in"):
         loads[name].wait()
     gain1, gain2 = s.gains[0:1, :], s.gains[1:2, :]
-    h_first, h_cot, h_out, h_grad = [Halo(s, i, i < 2) for i in range(4)]
+    share = TableShare(s)
     reduce2, reduce1 = Reduce(s, 1), Reduce(s, 0)
     cot = pack(field(s.cot_in), "n")
     x1 = nn(reorder("a", "n"), field(s.x_in))
     pl.semaphore_wait(barrier, expected)
+    share.start()
     h_cot.start(cot)
 
-    first = forward(s, 0, x1, gain1, s.wqkv, s.wproj, lambda g: s.bias1[...], 1)
+    attend(s, 0, x1, gain1, s.wqkv, lambda g: s.bias1[...], 1)
+    first = project(s, 0, x1, s.wproj, 1)
     h_first.start(pack(first, "a"))
-    expand_second(s, lat)
+    share.forward()
+    g2 = unpack(h_cot.finish(), "b").astype(BF16)
+    head_backs(s, 1, g2, s.wproj, 2)
+    share.finish()
+    expand_second(s, home()[0])
     x2 = unpack(h_first.finish(), "b")
-    second = forward(s, 1, x2, gain2, s.wqkv, s.wproj, lambda g: s.bias2[g], 2)
-    g2 = unpack(h_cot.finish(), "b").astype(BF16)
-    dh2, saved2 = backward(s, 1, g2, gain2, s.wqkv, s.wproj, 2)
+    attend(s, 1, x2, gain2, s.wqkv, lambda g: s.bias2[g], 2)
+    dh2, saved2 = backward(s, 1, g2, gain2, s.wqkv, 2)
     h_grad.start(pack(dh2, "b"))
-    h_out.start(pack(second, "b"))
+    h_out.start(pack(project(s, 1, x2, s.wproj, 2), "b"))
     gradients(s, 1, g2, saved2, fold_second(s), 2)
     reduce2.step(0)
     reduce2.step(1)
     g1 = unpack(h_grad.finish(), "a").astype(BF16)
-    dx, saved1 = backward(s, 0, g1, gain1, s.wqkv, s.wproj, 1)
+    head_backs(s, 0, g1, s.wproj, 1)
+    dx, saved1 = backward(s, 0, g1, gain1, s.wqkv, 1)
     reduce2.step(2)
     gradients(s, 0, g1, saved1, fold_first(s), 1)
     reduce1.step(0)

time: 80 us -> 76.4 us (0.955)
  Pallas kernels: 79.2 us -> 75.6 us
    pallas_call x1, Pallas kernels: 76.6 us -> 72.9 us  [body(): pl.pallas_call(main_kernel, out_shape=(field, field, jax.ShapeDtypeStruct...]
where the time goes in v4:
time: 76.4 us; the launch traced here: 76.2 us
  Pallas kernels  75.6 us (99%)
    pallas_call x1, Pallas kernels, body(): pl.pallas_call(main_kernel, out_shape=(field, field, jax.ShapeDtypeStruct...  72.9 us
    pallas_call x1, Pallas kernels, body(): pl.pallas_call(finish_kernel, out_shape=(field, field, jax.ShapeDtypeStru...  2.66 us

profile of v4, /device:TPU:1, one launch (start us, length us, event | category | flops | bytes accessed | tf_op | source)
XLA Modules:
  0.0 76.2 jit_solution(12177725174280517248)
XLA Ops:
  0.6 72.9 %both_blocks.1 = (bf16[6,12,2,192]{3,2,1,0:T(2,128)(2,1)}, bf16[6,12,2,192]{3,2,1,0:T(2,128)(2,1)}, bf16[2,2,20,48,128]{4,3,2,1,0:T(8,128)(2,1)}) custom-call(bf16[6,12,2,192]{3,2,1,0:T(2,128)(2,1)} %bitcast.7, bf16[6,12,2,192]{3,2,1,0:T(2,128)(2,1)} %bitcast.8, f32[2,192]{1,0:T(2,128)} %gains_ref.1, bf16[2,192,576]{2,1,0:T(8,128)(2,1)} %wqkv_ref.1, ...), custom_call_target="tpu_custom_call" | custom-call | tf_op jit(solution)/shard_map/both_blocks/pallas_call | solution.py:763
  73.6 2.7 %unpack.1 = (bf16[6,12,2,192]{3,2,1,0:T(2,128)(2,1)}, bf16[6,12,2,192]{3,2,1,0:T(2,128)(2,1)}, f32[2,192]{1,0:T(2,128)}, f32[2,192,576]{2,1,0:T(8,128)}, f32[2,1...) custom-call(bf16[2,2,20,48,128]{4,3,2,1,0:T(8,128)(2,1)} %get-tuple-element.15.red_ref, ...), custom_call_target="tpu_custom_call" | custom-call | tf_op jit(solution)/shard_map/unpack/pallas_call | solution.py:782

commit v5 on v3

--- a/solution.py
+++ b/solution.py
@@ -239,7 +239,7 @@
     return [nt(spread(512, 6, par, 1), s.wide[par, :, 0:512].astype(BF16)) for par in range(2)]
 
 
-def forward(s, j, x, gain, wqkv_ref, wproj_ref, bias, groups):
+def attend(s, j, x, gain, wqkv_ref, bias, groups):
     n = 144 // groups
     center = x - jnp.mean(x, -1, keepdims=True)
     inverse = lax.rsqrt(jnp.mean(center * center, -1, keepdims=True) + 1e-05)
@@ -252,7 +252,6 @@
     s.scaled[j] = scaled
     s.k[j] = k
     s.v[j] = v
-    attended = []
     for g in range(groups):
         rows = slice(g * n, g * n + n)
         qm = head_stack(q[rows])
@@ -261,20 +260,34 @@
         weight = jnp.exp(scores - jnp.max(scores, 0, keepdims=True))
         probs = weight * (1.0 / jnp.sum(weight, 0, keepdims=True))
         s.probs[j, rows, 0 : 6 * n] = probs
-        mixed_t = head_diagonal(tn(v[rows].astype(BF16), probs.astype(BF16)), n)
+
+
+def project(s, j, x, wproj_ref, groups):
+    n = 144 // groups
+    attended = []
+    for g in range(groups):
+        rows = slice(g * n, g * n + n)
+        v, probs = s.v[j, rows, :], s.probs[j, rows, 0 : 6 * n]
+        mixed_t = head_diagonal(tn(v.astype(BF16), probs.astype(BF16)), n)
         s.mixed_t[j, g, :, 0:n] = mixed_t
         attended.append(tn(mixed_t.astype(BF16), wproj_ref[j]))
     att = attended[0] if groups == 1 else jnp.concatenate(attended, 0)
     return (x + att).astype(BF16)
 
 
-def backward(s, j, g_in, gain, wqkv_ref, wproj_ref, groups):
+def head_backs(s, j, g_in, wproj_ref, groups):
     n = 144 // groups
     back = nt(g_in, wproj_ref[j])
+    for g in range(groups):
+        s.backm[j, g * 6 * n : (g + 1) * 6 * n, :] = head_stack(back[g * n : g * n + n])
+
+
+def backward(s, j, groups):
+    n = 144 // groups
     dqs, dks, dvs = [], [], []
     for g in range(groups):
         rows = slice(g * n, g * n + n)
-        backm = head_stack(back[rows])
+        backm = s.backm[j, g * 6 * n : (g + 1) * 6 * n, :]
         probs = s.probs[j, rows, 0 : 6 * n]
         k = s.k[j, rows, :].astype(BF16)
         v = s.v[j, rows, :].astype(BF16)
@@ -290,9 +303,12 @@
         dq, dk, dv = dqs[0], dks[0], dvs[0]
     else:
         dq, dk, dv = [jnp.concatenate(p, 0) for p in (dqs, dks, dvs)]
-    dq, dk, dv = dq.astype(BF16), dk.astype(BF16), dv.astype(BF16)
+    return dq.astype(BF16), dk.astype(BF16), dv.astype(BF16)
+
+
+def norm_backward(s, j, g_in, d_packed, gain, wqkv_ref):
     w = wqkv_ref[j]
-    d_scaled = nt(dq, w[:, 0:192]) + nt(dk, w[:, 192:384]) + nt(dv, w[:, 384:576])
+    d_scaled = sum(nt(d_packed[i], w[:, 192 * i : 192 * i + 192]) for i in range(3))
     normed = s.normed[j]
     d_normed = d_scaled * gain
     d_hidden = s.inverse[j] * (
@@ -300,30 +316,31 @@
         - jnp.mean(d_normed, -1, keepdims=True)
         - normed * jnp.mean(d_normed * normed, -1, keepdims=True)
     )
-    result = (g_in.astype(F32) + d_hidden).astype(BF16)
-    return result, (dq, dk, dv, d_scaled)
-
-
-def gradients(s, j, g_in, saved, folded, groups):
+    return (g_in.astype(F32) + d_hidden).astype(BF16), d_scaled
+
+
+def weight_gradients(s, j, g_in, d_packed, groups):
     n = 144 // groups
-    dq, dk, dv, d_scaled = saved
     scaled = s.scaled[j]
-    s.grad[:, 0:192] = tn(scaled, dq)
-    s.grad[:, 192:384] = tn(scaled, dk)
-    s.grad[:, 384:576] = tn(scaled, dv)
+    for i, part in enumerate(d_packed):
+        s.grad[:, 192 * i : 192 * i + 192] = tn(scaled, part)
     d_proj = jnp.zeros((192, 192), F32)
     for g in range(groups):
         d_proj = d_proj + nn(
             s.mixed_t[j, g, :, 0:n].astype(BF16), g_in[g * n : g * n + n]
         )
     s.grad[:, 576:768] = d_proj
+    for half in range(2):
+        for slot in range(12):
+            column, row = half * 384 + (slot // 4) * 128, (slot % 4) * 48
+            s.payload[j, half, slot] = s.grad[row : row + 48, column : column + 128].astype(BF16)
+
+
+def other_gradients(s, j, d_scaled, folded):
     for h in range(HEADS):
         s.extra[24 * h : 24 * h + 24, 0:144] = folded[h % 2][24 * (h // 2) : 24 * (h // 2) + 24]
     s.extra[144:145, 0:192] = jnp.sum(d_scaled * s.normed[j], 0, keepdims=True)
     for half in range(2):
-        for slot in range(12):
-            column, row = half * 384 + (slot // 4) * 128, (slot % 4) * 48
-            s.payload[j, half, slot] = s.grad[row : row + 48, column : column + 128].astype(BF16)
         for slot, row in ((12, 144), (13, 0), (14, 48), (15, 96)):
             s.payload[j, half, slot] = s.extra[
                 row : row + 48, 128 * half : 128 * half + 128
@@ -333,38 +350,43 @@
 class Halo:
     def __init__(self, s, which, forward_shift):
         lat, lon = lax.axis_index("lat"), lax.axis_index("lon")
+        home_lat, home_lon = runs_at(lat, lon)
         nlat, nlon = lax.axis_size("lat"), lax.axis_size("lon")
         self.s, self.which = s, which
-        self.copies = []
-        self.stay = 3 if forward_shift else 0
-        for i, quarter in enumerate(q for q in range(4) if q != self.stay):
+        self.copies, self.partners = [], []
+        for quarter in range(4):
+            down, right = quarter // 2, quarter % 2
             if forward_shift:
-                by_lat, by_lon = quarter // 2 - 1 + nlat, quarter % 2 - 1 + nlon
+                peer = runs_at(
+                    lax.rem(lat + down - 1 + nlat, nlat), lax.rem(lon + right - 1 + nlon, nlon)
+                )
             else:
-                by_lat, by_lon = quarter // 2, quarter % 2
+                peer = lax.rem(home_lat + down, nlat), lax.rem(home_lon + right, nlon)
+            self.partners.append(peer)
             self.copies.append(
                 pltpu.make_async_remote_copy(
                     src_ref=s.halo_out.at[which, quarter],
                     dst_ref=s.halo_in.at[which, 3 - quarter],
-                    send_sem=s.halo_send.at[which, i],
-                    recv_sem=s.halo_recv.at[which, i],
-                    device_id=(lax.rem(lat + by_lat, nlat), lax.rem(lon + by_lon, nlon)),
+                    send_sem=s.halo_send.at[which, quarter],
+                    recv_sem=s.halo_recv.at[which, quarter],
+                    device_id=peer,
                     device_id_type=MESH,
                 )
             )
 
     def start(self, quarters):
-        for q in range(4):
-            self.s.halo_out[self.which, q] = quarters[64 * q : 64 * q + 64]
+        self.s.halo_out[self.which] = quarters.reshape(4, 64, 128)
         for copy in self.copies:
             copy.start()
-        stay = self.stay
-        self.s.halo_in[self.which, 3 - stay] = quarters[64 * stay : 64 * stay + 64]
 
     def finish(self):
         for copy in self.copies:
-            copy.wait()
+            copy.wait_recv()
         return self.s.halo_in[self.which].reshape(256, 128)
+
+    def sent(self):
+        for copy in self.copies:
+            copy.wait_send()
 
 
 def place():
@@ -373,6 +395,10 @@
     return lat, lon, lat // 2, lax.rem(lat, 2), lon // 8, line // 2, lax.rem(line, 2)
 
 
+def runs_at(lat, lon):
+    return lat, lax.rem(lon + 32, 64)
+
+
 def sibling():
     lat, lon, y, zh, zl, x, core = place()
     return lat, zl * 8 + x * 2 + 1 - core
@@ -380,12 +406,12 @@
 
 def plane_peers():
     lat, lon, y, zh, zl, x, core = place()
+    hops = lambda step: min(step, 4 - step)
+    steps = [(dx, dy) for dy in range(4) for dx in range(4) if dx or dy]
     out = []
-    for dy in range(4):
-        for dx in range(4):
-            if dx or dy:
-                py, px = lax.rem(y + dy, 4), lax.rem(x + dx, 4)
-                out.append((dx if dy == 0 else 0, (py * 2 + zh, zl * 8 + px * 2 + core), py * 4 + px))
+    for dx, dy in sorted(steps, key=lambda step: -hops(step[0]) - hops(step[1])):
+        py, px = lax.rem(y + dy, 4), lax.rem(x + dx, 4)
+        out.append((dx if dy == 0 else 0, (py * 2 + zh, zl * 8 + px * 2 + core), py * 4 + px))
     return out
 
 
@@ -418,7 +444,12 @@
         self.used = 0
         own, table = self.own, 16 + x
         near, far, half = self.near, self.far, self.half
-        stages = [[self.copy(s.payload.at[j, 1 - core], s.in_core.at[j], sibling())], [], [], [], []]
+        stages = [[], [], [], [], []]
+        for first, count in ((0, 12), (12, 4)):
+            slots = pl.ds(first, count)
+            stages[0].append(
+                self.copy(s.payload.at[j, 1 - core, slots], s.in_core.at[j, slots], sibling())
+            )
         for i, (dx, peer, slot) in enumerate(plane_peers()):
             stages[1].append(self.copy(s.half.at[j, slot], s.in_plane.at[j, i], peer))
             stages[4].append(self.copy(s.red.at[j, core, own], s.red.at[j, core, own], peer))
@@ -451,7 +482,7 @@
         s, j, core = self.s, self.j, self.core
         if number > 0:
             for copy in self.stages[number - 1]:
-                copy.wait()
+                copy.wait_recv()
         if number == 1:
             for slot in range(16):
                 total = s.payload[j, core, slot].astype(F32) + s.in_core[j, slot].astype(F32)
@@ -478,20 +509,19 @@
             s.red[j, core, self.own] = total.astype(BF16)
             table = s.far_tab[j, 0].astype(F32) + s.far_tab[j, 1].astype(F32)
             s.red[j, core, 16 + self.x] = table.astype(BF16)
-        if number < 6:
+        if 0 < number < 6:
             for copy in self.stages[number]:
                 copy.start()
-
-
-def signal_partners():
+        if number > 0:
+            for copy in self.stages[number - 1]:
+                copy.wait_send()
+
+
+def signal_partners(halos):
     barrier = pltpu.get_barrier_semaphore()
-    lat, lon = lax.axis_index("lat"), lax.axis_index("lon")
-    nlat, nlon = lax.axis_size("lat"), lax.axis_size("lon")
-    partners = [sibling()] + near_peers() + far_peers() + [p for _, p, _ in plane_peers()]
-    partners.append(half_peer())
-    for da, db in ((0, 1), (1, 0), (1, 1)):
-        partners.append((lax.rem(lat + da, nlat), lax.rem(lon + db, nlon)))
-        partners.append((lax.rem(lat - da + nlat, nlat), lax.rem(lon - db + nlon, nlon)))
+    partners = halos[0].partners + halos[-1].partners
+    partners += far_peers() + near_peers() + [p for _, p, _ in plane_peers()]
+    partners += [sibling(), half_peer()]
     for partner in partners:
         pl.semaphore_signal(barrier, inc=1, device_id=partner, device_id_type=MESH)
     return barrier, len(partners)
@@ -520,6 +550,7 @@
     k=pltpu.VMEM((2, 144, 192), F32),
     v=pltpu.VMEM((2, 144, 192), F32),
     qm=pltpu.VMEM((2, 864, 192), BF16),
+    backm=pltpu.VMEM((2, 864, 192), BF16),
     probs=pltpu.VMEM((2, 144, 864), F32),
     mixed_t=pltpu.VMEM((2, 2, 192, 144), F32),
     grad=pltpu.VMEM((192, 768), F32),
@@ -534,10 +565,10 @@
     far=pltpu.VMEM((2, 4, 48, 128), BF16),
     far_tab=pltpu.VMEM((2, 2, 48, 128), BF16),
     red=pltpu.VMEM((2, 2, 20, 48, 128), BF16),
-    halo_send=pltpu.SemaphoreType.DMA((4, 3)),
-    halo_recv=pltpu.SemaphoreType.DMA((4, 3)),
-    ar_send=pltpu.SemaphoreType.DMA((2, 45)),
-    ar_recv=pltpu.SemaphoreType.DMA((2, 45)),
+    halo_send=pltpu.SemaphoreType.DMA((4, 4)),
+    halo_recv=pltpu.SemaphoreType.DMA((4, 4)),
+    ar_send=pltpu.SemaphoreType.DMA((2, 48)),
+    ar_recv=pltpu.SemaphoreType.DMA((2, 48)),
 )
 
 
@@ -563,7 +594,9 @@
     }
     for load in loads.values():
         load.start()
-    barrier, expected = signal_partners()
+    h_first, h_cot, h_out, h_grad = halos = [Halo(s, i, i < 2) for i in range(4)]
+    barrier, expected = signal_partners(halos)
+    reduce2, reduce1 = Reduce(s, 1), Reduce(s, 0)
 
     s.tab[...] = jnp.zeros((6, 24, 144), F32)
     s.ds[:, 768:1024] = jnp.zeros((144, 256), F32)
@@ -579,41 +612,50 @@
         copy.start()
         return copy
 
-    for name in ("tab_in", "pad"):
-        loads[name].wait()
+    for load in loads.values():
+        load.wait()
+    gain1, gain2 = s.gains[0:1, :], s.gains[1:2, :]
+    x1 = nn(reorder("a", "n"), field(s.x_in))
     expand_first(s, lat)
-    for name in ("x_in", "gains", "wqkv", "wproj", "cot_in"):
-        loads[name].wait()
-    gain1, gain2 = s.gains[0:1, :], s.gains[1:2, :]
-    h_first, h_cot, h_out, h_grad = [Halo(s, i, i < 2) for i in range(4)]
-    reduce2, reduce1 = Reduce(s, 1), Reduce(s, 0)
+    attend(s, 0, x1, gain1, s.wqkv, lambda g: s.bias1[...], 1)
+    first = pack(project(s, 0, x1, s.wproj, 1), "a")
     cot = pack(field(s.cot_in), "n")
-    x1 = nn(reorder("a", "n"), field(s.x_in))
     pl.semaphore_wait(barrier, expected)
+    h_first.start(first)
     h_cot.start(cot)
 
-    first = forward(s, 0, x1, gain1, s.wqkv, s.wproj, lambda g: s.bias1[...], 1)
-    h_first.start(pack(first, "a"))
     expand_second(s, lat)
+    g2 = unpack(h_cot.finish(), "b").astype(BF16)
+    head_backs(s, 1, g2, s.wproj, 2)
     x2 = unpack(h_first.finish(), "b")
-    second = forward(s, 1, x2, gain2, s.wqkv, s.wproj, lambda g: s.bias2[g], 2)
-    g2 = unpack(h_cot.finish(), "b").astype(BF16)
-    dh2, saved2 = backward(s, 1, g2, gain2, s.wqkv, s.wproj, 2)
+    attend(s, 1, x2, gain2, s.wqkv, lambda g: s.bias2[g], 2)
+    d_packed = backward(s, 1, 2)
+    dh2, d_scaled = norm_backward(s, 1, g2, d_packed, gain2, s.wqkv)
     h_grad.start(pack(dh2, "b"))
-    h_out.start(pack(second, "b"))
-    gradients(s, 1, g2, saved2, fold_second(s), 2)
-    reduce2.step(0)
+    h_out.start(pack(project(s, 1, x2, s.wproj, 2), "b"))
+    weight_gradients(s, 1, g2, d_packed, 2)
+    reduce2.stages[0][0].start()
+    other_gradients(s, 1, d_scaled, fold_second(s))
+    reduce2.stages[0][1].start()
+    h_cot.sent()
+    h_first.sent()
     reduce2.step(1)
     g1 = unpack(h_grad.finish(), "a").astype(BF16)
-    dx, saved1 = backward(s, 0, g1, gain1, s.wqkv, s.wproj, 1)
+    head_backs(s, 0, g1, s.wproj, 1)
+    d_packed = backward(s, 0, 1)
+    weight_gradients(s, 0, g1, d_packed, 1)
+    reduce1.stages[0][0].start()
+    dx, d_scaled = norm_backward(s, 0, g1, d_packed, gain1, s.wqkv)
+    other_gradients(s, 0, d_scaled, fold_first(s))
+    reduce1.stages[0][1].start()
     reduce2.step(2)
-    gradients(s, 0, g1, saved1, fold_first(s), 1)
-    reduce1.step(0)
+    reduce1.step(1)
     s.dx[...] = nn(reorder("n", "a"), dx).reshape(6, 12, 2, 192).astype(BF16)
     stores = [store(0, s.dx, dx_ref)]
-    reduce1.step(1)
     s.out[...] = unpack(h_out.finish(), "n").reshape(6, 12, 2, 192).astype(BF16)
     stores.append(store(1, s.out, out_ref))
+    h_grad.sent()
+    h_out.sent()
     reduce2.step(3)
     reduce1.step(2)
     reduce2.step(4)

time: 80 us -> 72.5 us (0.906)
  Pallas kernels: 79.2 us -> 71.6 us
    pallas_call x1, Pallas kernels: 76.6 us -> 69 us  [body(): pl.pallas_call(main_kernel, out_shape=(field, field, jax.ShapeDtypeStruct...]
where the time goes in v5:
time: 72.5 us; the launch traced here: 72.3 us
  Pallas kernels  71.6 us (99%)
    pallas_call x1, Pallas kernels, body(): pl.pallas_call(main_kernel, out_shape=(field, field, jax.ShapeDtypeStruct...  69 us
    pallas_call x1, Pallas kernels, body(): pl.pallas_call(finish_kernel, out_shape=(field, field, jax.ShapeDtypeStru...  2.66 us

profile of v5, /device:TPU:1, one launch (start us, length us, event | category | flops | bytes accessed | tf_op | source)
XLA Modules:
  0.0 72.3 jit_solution(15898275671734445593)
XLA Ops:
  0.6 69.0 %both_blocks.1 = (bf16[6,12,2,192]{3,2,1,0:T(2,128)(2,1)}, bf16[6,12,2,192]{3,2,1,0:T(2,128)(2,1)}, bf16[2,2,20,48,128]{4,3,2,1,0:T(8,128)(2,1)}) custom-call(bf16[6,12,2,192]{3,2,1,0:T(2,128)(2,1)} %bitcast.7, bf16[6,12,2,192]{3,2,1,0:T(2,128)(2,1)} %bitcast.8, f32[2,192]{1,0:T(2,128)} %gains_ref.1, bf16[2,192,576]{2,1,0:T(8,128)(2,1)} %wqkv_ref.1, ...), custom_call_target="tpu_custom_call" | custom-call | tf_op jit(solution)/shard_map/both_blocks/pallas_call | solution.py:715
  69.6 2.7 %unpack.1 = (bf16[6,12,2,192]{3,2,1,0:T(2,128)(2,1)}, bf16[6,12,2,192]{3,2,1,0:T(2,128)(2,1)}, f32[2,192]{1,0:T(2,128)}, f32[2,192,576]{2,1,0:T(8,128)}, f32[2,1...) custom-call(bf16[2,2,20,48,128]{4,3,2,1,0:T(8,128)(2,1)} %get-tuple-element.15.red_ref, ...), custom_call_target="tpu_custom_call" | custom-call | tf_op jit(solution)/shard_map/unpack/pallas_call | solution.py:734

commit v6 on v5

--- a/solution.py
+++ b/solution.py
@@ -367,12 +367,20 @@
                 pltpu.make_async_remote_copy(
                     src_ref=s.halo_out.at[which, quarter],
                     dst_ref=s.halo_in.at[which, 3 - quarter],
-                    send_sem=s.halo_send.at[which, quarter],
-                    recv_sem=s.halo_recv.at[which, quarter],
+                    send_sem=s.halo_send.at[which],
+                    recv_sem=s.halo_recv.at[which],
                     device_id=peer,
                     device_id_type=MESH,
                 )
             )
+        self.all = pltpu.make_async_remote_copy(
+            src_ref=s.halo_out.at[which],
+            dst_ref=s.halo_in.at[which],
+            send_sem=s.halo_send.at[which],
+            recv_sem=s.halo_recv.at[which],
+            device_id=self.partners[0],
+            device_id_type=MESH,
+        )
 
     def start(self, quarters):
         self.s.halo_out[self.which] = quarters.reshape(4, 64, 128)
@@ -380,13 +388,11 @@
             copy.start()
 
     def finish(self):
-        for copy in self.copies:
-            copy.wait_recv()
+        self.all.wait_recv()
         return self.s.halo_in[self.which].reshape(256, 128)
 
     def sent(self):
-        for copy in self.copies:
-            copy.wait_send()
+        self.all.wait_send()
 
 
 def place():
@@ -441,34 +447,39 @@
         self.s, self.j, self.core, self.x = s, j, core, x
         self.own = y * 4 + x
         self.near, self.far, self.half = lax.rem(zl, 4), zh * 2 + zl // 4, zl // 4
-        self.used = 0
         own, table = self.own, 16 + x
         near, far, half = self.near, self.far, self.half
-        stages = [[], [], [], [], []]
+        stages = [[] for _ in range(6)]
+
+        def add(number, src, dst, peer):
+            stages[number].append(self.copy(number, src, dst, peer))
+
         for first, count in ((0, 12), (12, 4)):
             slots = pl.ds(first, count)
-            stages[0].append(
-                self.copy(s.payload.at[j, 1 - core, slots], s.in_core.at[j, slots], sibling())
-            )
+            add(0, s.payload.at[j, 1 - core, slots], s.in_core.at[j, slots], sibling())
         for i, (dx, peer, slot) in enumerate(plane_peers()):
-            stages[1].append(self.copy(s.half.at[j, slot], s.in_plane.at[j, i], peer))
-            stages[4].append(self.copy(s.red.at[j, core, own], s.red.at[j, core, own], peer))
+            add(1, s.half.at[j, slot], s.in_plane.at[j, i], peer)
+            add(4, s.red.at[j, core, own], s.red.at[j, core, own], peer)
             if dx:
                 px = lax.rem(x + dx, 4)
-                stages[1].append(self.copy(s.half.at[j, 13 + px], s.in_plane.at[j, 14 + dx], peer))
-                stages[4].append(
-                    self.copy(s.red.at[j, core, table], s.red.at[j, core, table], peer)
-                )
+                add(1, s.half.at[j, 13 + px], s.in_plane.at[j, 14 + dx], peer)
+                add(4, s.red.at[j, core, table], s.red.at[j, core, table], peer)
         for peer in near_peers():
-            stages[2].append(self.copy(s.near.at[j, near], s.near.at[j, near], peer))
+            add(2, s.near.at[j, near], s.near.at[j, near], peer)
         for peer in far_peers():
-            stages[3].append(self.copy(s.far.at[j, far], s.far.at[j, far], peer))
-        stages[3].append(self.copy(s.far_tab.at[j, half], s.far_tab.at[j, half], half_peer()))
-        stages.append([self.copy(s.red.at[j, core], s.red.at[j, core], sibling())])
+            add(3, s.far.at[j, far], s.far.at[j, far], peer)
+        add(3, s.far_tab.at[j, half], s.far_tab.at[j, half], half_peer())
+        for first, count in ((0, 13), (16, 3)):
+            slots = pl.ds(first, count)
+            add(5, s.red.at[j, core, slots], s.red.at[j, core, slots], sibling())
         self.stages = stages
-
-    def copy(self, src, dst, peer):
-        number, self.used = self.used, self.used + 1
+        sizes = (
+            s.in_core.at[j], s.in_plane.at[j], s.near.at[j, pl.ds(0, 3)], s.far.at[j],
+            s.red.at[j, core, pl.ds(0, 18)], s.red.at[j, core, pl.ds(0, 16)],
+        )
+        self.all = [self.copy(i, size, size, sibling()) for i, size in enumerate(sizes)]
+
+    def copy(self, number, src, dst, peer):
         return pltpu.make_async_remote_copy(
             src_ref=src,
             dst_ref=dst,
@@ -481,8 +492,7 @@
     def step(self, number):
         s, j, core = self.s, self.j, self.core
         if number > 0:
-            for copy in self.stages[number - 1]:
-                copy.wait_recv()
+            self.all[number - 1].wait_recv()
         if number == 1:
             for slot in range(16):
                 total = s.payload[j, core, slot].astype(F32) + s.in_core[j, slot].astype(F32)
@@ -513,15 +523,15 @@
             for copy in self.stages[number]:
                 copy.start()
         if number > 0:
-            for copy in self.stages[number - 1]:
-                copy.wait_send()
+            self.all[number - 1].wait_send()
 
 
 def signal_partners(halos):
     barrier = pltpu.get_barrier_semaphore()
     partners = halos[0].partners + halos[-1].partners
-    partners += far_peers() + near_peers() + [p for _, p, _ in plane_peers()]
-    partners += [sibling(), half_peer()]
+    ahead, opposite, behind = far_peers()
+    partners += [ahead, behind] + [p for _, p, _ in plane_peers()] + near_peers()
+    partners += [half_peer(), sibling()]
     for partner in partners:
         pl.semaphore_signal(barrier, inc=1, device_id=partner, device_id_type=MESH)
     return barrier, len(partners)
@@ -538,7 +548,7 @@
     loads=pltpu.SemaphoreType.DMA((7,)),
     out=pltpu.VMEM((6, 12, 2, 192), BF16),
     dx=pltpu.VMEM((6, 12, 2, 192), BF16),
-    stores=pltpu.SemaphoreType.DMA((4,)),
+    stores=pltpu.SemaphoreType.DMA((5,)),
     tab=pltpu.VMEM((6, 24, 144), F32),
     wide=pltpu.VMEM((2, 144, 1024), F32),
     bias1=pltpu.VMEM((144, 864), F32),
@@ -565,10 +575,11 @@
     far=pltpu.VMEM((2, 4, 48, 128), BF16),
     far_tab=pltpu.VMEM((2, 2, 48, 128), BF16),
     red=pltpu.VMEM((2, 2, 20, 48, 128), BF16),
-    halo_send=pltpu.SemaphoreType.DMA((4, 4)),
-    halo_recv=pltpu.SemaphoreType.DMA((4, 4)),
-    ar_send=pltpu.SemaphoreType.DMA((2, 48)),
-    ar_recv=pltpu.SemaphoreType.DMA((2, 48)),
+    relay=pltpu.SemaphoreType.REGULAR,
+    halo_send=pltpu.SemaphoreType.DMA((4,)),
+    halo_recv=pltpu.SemaphoreType.DMA((4,)),
+    ar_send=pltpu.SemaphoreType.DMA((2, 6)),
+    ar_recv=pltpu.SemaphoreType.DMA((2, 6)),
 )
 
 
@@ -619,15 +630,16 @@
     expand_first(s, lat)
     attend(s, 0, x1, gain1, s.wqkv, lambda g: s.bias1[...], 1)
     first = pack(project(s, 0, x1, s.wproj, 1), "a")
-    cot = pack(field(s.cot_in), "n")
     pl.semaphore_wait(barrier, expected)
     h_first.start(first)
-    h_cot.start(cot)
+    pl.semaphore_signal(s.relay, inc=1, device_id=far_peers()[2], device_id_type=MESH)
+    h_cot.start(pack(field(s.cot_in), "n"))
 
     expand_second(s, lat)
     g2 = unpack(h_cot.finish(), "b").astype(BF16)
     head_backs(s, 1, g2, s.wproj, 2)
     x2 = unpack(h_first.finish(), "b")
+    pl.semaphore_wait(s.relay, 1)
     attend(s, 1, x2, gain2, s.wqkv, lambda g: s.bias2[g], 2)
     d_packed = backward(s, 1, 2)
     dh2, d_scaled = norm_backward(s, 1, g2, d_packed, gain2, s.wqkv)
@@ -648,8 +660,8 @@
     dx, d_scaled = norm_backward(s, 0, g1, d_packed, gain1, s.wqkv)
     other_gradients(s, 0, d_scaled, fold_first(s))
     reduce1.stages[0][1].start()
+    reduce1.step(1)
     reduce2.step(2)
-    reduce1.step(1)
     s.dx[...] = nn(reorder("n", "a"), dx).reshape(6, 12, 2, 192).astype(BF16)
     stores = [store(0, s.dx, dx_ref)]
     s.out[...] = unpack(h_out.finish(), "n").reshape(6, 12, 2, 192).astype(BF16)
@@ -658,15 +670,17 @@
     h_out.sent()
     reduce2.step(3)
     reduce1.step(2)
+    reduce1.step(3)
     reduce2.step(4)
-    reduce1.step(3)
+    reduce1.step(4)
     reduce2.step(5)
-    reduce1.step(4)
     reduce2.step(6)
     stores.append(store(2, s.red.at[1], red_ref.at[1]))
     reduce1.step(5)
+    core = reduce1.core
+    stores.append(store(3, s.red.at[0, core], red_ref.at[0, core]))
     reduce1.step(6)
-    stores.append(store(3, s.red.at[0], red_ref.at[0]))
+    stores.append(store(4, s.red.at[0, 1 - core], red_ref.at[0, 1 - core]))
     for copy in stores:
         copy.wait()
 

time: 72.5 us -> 70.1 us (0.967)
  Pallas kernels: 71.6 us -> 69.3 us
    pallas_call x1, Pallas kernels: 69 us -> 66.6 us  [body(): pl.pallas_call(main_kernel, out_shape=(field, field, jax.ShapeDtypeStruct...]
where the time goes in v6:
time: 70.1 us; the launch traced here: 69.9 us
  Pallas kernels  69.3 us (99%)
    pallas_call x1, Pallas kernels, body(): pl.pallas_call(main_kernel, out_shape=(field, field, jax.ShapeDtypeStruct...  66.6 us
    pallas_call x1, Pallas kernels, body(): pl.pallas_call(finish_kernel, out_shape=(field, field, jax.ShapeDtypeStru...  2.66 us

profile of v6, /device:TPU:1, one launch (start us, length us, event | category | flops | bytes accessed | tf_op | source)
XLA Modules:
  0.0 69.9 jit_solution(723540368514466048)
XLA Ops:
  0.6 66.6 %both_blocks.1 = (bf16[6,12,2,192]{3,2,1,0:T(2,128)(2,1)}, bf16[6,12,2,192]{3,2,1,0:T(2,128)(2,1)}, bf16[2,2,20,48,128]{4,3,2,1,0:T(8,128)(2,1)}) custom-call(bf16[6,12,2,192]{3,2,1,0:T(2,128)(2,1)} %bitcast.7, bf16[6,12,2,192]{3,2,1,0:T(2,128)(2,1)} %bitcast.8, f32[2,192]{1,0:T(2,128)} %gains_ref.1, bf16[2,192,576]{2,1,0:T(8,128)(2,1)} %wqkv_ref.1, ...), custom_call_target="tpu_custom_call" | custom-call | tf_op jit(solution)/shard_map/both_blocks/pallas_call | solution.py:729
  67.3 2.7 %unpack.1 = (bf16[6,12,2,192]{3,2,1,0:T(2,128)(2,1)}, bf16[6,12,2,192]{3,2,1,0:T(2,128)(2,1)}, f32[2,192]{1,0:T(2,128)}, f32[2,192,576]{2,1,0:T(8,128)}, f32[2,1...) custom-call(bf16[2,2,20,48,128]{4,3,2,1,0:T(8,128)(2,1)} %get-tuple-element.15.red_ref, ...), custom_call_target="tpu_custom_call" | custom-call | tf_op jit(solution)/shard_map/unpack/pallas_call | solution.py:748

commit v7 on v6

--- a/solution.py
+++ b/solution.py
@@ -64,6 +64,9 @@
     return jnp.where(inner >= 18, quarter + 18 + inner, -1)
 
 
+SLOTS = ("s", "s1", "s2")
+
+
 def reorder(to, of):
     n, m = [256 if order[0] == "s" else 144 for order in (to, of)]
     l, r, c, used = tokens_of(to, n)
@@ -71,16 +74,17 @@
     return jnp.where(place == lax.broadcasted_iota(jnp.int32, (n, m), 1), 1.0, 0.0).astype(BF16)
 
 
-def pack(x, order):
+def pack(x, order, ready=None):
     wide, rest = x[:, 0:128], x[:, 128:192]
-    pairs = [nn(reorder(to, order), rest) for to in ("s1", "s2")]
-    return (nn(reorder("s", order), wide) + jnp.concatenate(pairs, 1)).astype(BF16)
-
-
-def unpack(x, order):
-    left, right = nn(reorder(order, "s1"), x), nn(reorder(order, "s2"), x)
-    rest = left[:, 0:64] + right[:, 64:128]
-    return jnp.concatenate([nn(reorder(order, "s"), x), rest], 1)
+    whole, first, second = ready or [reorder(to, order) for to in SLOTS]
+    pairs = jnp.concatenate([nn(first, rest), nn(second, rest)], 1)
+    return (nn(whole, wide) + pairs).astype(BF16)
+
+
+def unpack(x, order, ready=None):
+    whole, first, second = ready or [reorder(order, of) for of in SLOTS]
+    rest = nn(first, x)[:, 0:64] + nn(second, x)[:, 64:128]
+    return jnp.concatenate([nn(whole, x), rest], 1)
 
 
 def spread(lanes, step, par, parts):
@@ -427,13 +431,26 @@
     return [(lat, (quad + lax.rem(zl + d, 4)) * 8 + x * 2 + core) for d in range(1, 4)]
 
 
-def far_peers():
+def at_z(z):
     lat, lon, y, zh, zl, x, core = place()
-    out = []
-    for d in range(1, 4):
-        z = lax.rem(zh * 8 + zl + 4 * d, 16)
-        out.append((y * 2 + z // 8, lax.rem(z, 8) * 8 + x * 2 + core))
-    return out
+    z = lax.rem(z, 16)
+    return y * 2 + z // 8, lax.rem(z, 8) * 8 + x * 2 + core
+
+
+def quad_ends():
+    lat, lon, y, zh, zl, x, core = place()
+    quad, member = zh * 2 + zl // 4, lax.rem(zl, 4)
+    low = member == 0
+    is_end = low | (member == 3)
+    beside, across = quad + jnp.where(low, 3, 1), quad + 2
+    sends = [at_z(4 * beside + i) for i in range(4)]
+    sends += [at_z(4 * across + jnp.where(low, 2, 0) + i) for i in range(2)]
+    takes = [
+        at_z(4 * across + jnp.where(member < 2, 3, 0)),
+        at_z(4 * (quad + 1)),
+        at_z(4 * (quad + 3) + 3),
+    ]
+    return is_end, sends, takes
 
 
 def half_peer():
@@ -466,15 +483,16 @@
                 add(4, s.red.at[j, core, table], s.red.at[j, core, table], peer)
         for peer in near_peers():
             add(2, s.near.at[j, near], s.near.at[j, near], peer)
-        for peer in far_peers():
+        self.is_end, sends, _ = quad_ends()
+        for peer in sends:
             add(3, s.far.at[j, far], s.far.at[j, far], peer)
-        add(3, s.far_tab.at[j, half], s.far_tab.at[j, half], half_peer())
+        self.far_tab = self.copy(6, s.far_tab.at[j, half], s.far_tab.at[j, half], half_peer())
         for first, count in ((0, 13), (16, 3)):
             slots = pl.ds(first, count)
             add(5, s.red.at[j, core, slots], s.red.at[j, core, slots], sibling())
         self.stages = stages
         sizes = (
-            s.in_core.at[j], s.in_plane.at[j], s.near.at[j, pl.ds(0, 3)], s.far.at[j],
+            s.in_core.at[j], s.in_plane.at[j], s.near.at[j, pl.ds(0, 3)], s.far.at[j, pl.ds(0, 3)],
             s.red.at[j, core, pl.ds(0, 18)], s.red.at[j, core, pl.ds(0, 16)],
         )
         self.all = [self.copy(i, size, size, sibling()) for i, size in enumerate(sizes)]
@@ -493,6 +511,8 @@
         s, j, core = self.s, self.j, self.core
         if number > 0:
             self.all[number - 1].wait_recv()
+        if number == 4:
+            self.far_tab.wait_recv()
         if number == 1:
             for slot in range(16):
                 total = s.payload[j, core, slot].astype(F32) + s.in_core[j, slot].astype(F32)
@@ -519,22 +539,39 @@
             s.red[j, core, self.own] = total.astype(BF16)
             table = s.far_tab[j, 0].astype(F32) + s.far_tab[j, 1].astype(F32)
             s.red[j, core, 16 + self.x] = table.astype(BF16)
-        if 0 < number < 6:
+        if number == 3:
+            self.far_tab.start()
+
+            @pl.when(self.is_end)
+            def _():
+                for copy in self.stages[3]:
+                    copy.start()
+
+        elif 0 < number < 6:
             for copy in self.stages[number]:
                 copy.start()
-        if number > 0:
+        if number == 4:
+            self.far_tab.wait_send()
+            size = s.in_plane.at[j, pl.ds(0, 6)]
+
+            @pl.when(self.is_end)
+            def _():
+                self.copy(3, size, size, sibling()).wait_send()
+
+        elif number > 0:
             self.all[number - 1].wait_send()
 
 
 def signal_partners(halos):
     barrier = pltpu.get_barrier_semaphore()
     partners = halos[0].partners + halos[-1].partners
-    ahead, opposite, behind = far_peers()
-    partners += [ahead, behind] + [p for _, p, _ in plane_peers()] + near_peers()
-    partners += [half_peer(), sibling()]
+    is_end, sends, takes = quad_ends()
+    partners += [p for _, p, _ in plane_peers()] + near_peers() + [half_peer(), sibling()]
+    expected = len(partners) + jnp.where(is_end, len(sends), 0)
+    partners += takes
     for partner in partners:
         pl.semaphore_signal(barrier, inc=1, device_id=partner, device_id_type=MESH)
-    return barrier, len(partners)
+    return barrier, expected
 
 
 SCRATCH = dict(
@@ -565,6 +602,8 @@
     mixed_t=pltpu.VMEM((2, 2, 192, 144), F32),
     grad=pltpu.VMEM((192, 768), F32),
     extra=pltpu.VMEM((192, 256), F32),
+    to_slots=pltpu.VMEM((3, 256, 144), BF16),
+    from_slots=pltpu.VMEM((6, 144, 256), BF16),
     halo_out=pltpu.VMEM((4, 4, 64, 128), BF16),
     halo_in=pltpu.VMEM((4, 4, 64, 128), BF16),
     payload=pltpu.VMEM((2, 2, 16, 48, 128), BF16),
@@ -575,11 +614,10 @@
     far=pltpu.VMEM((2, 4, 48, 128), BF16),
     far_tab=pltpu.VMEM((2, 2, 48, 128), BF16),
     red=pltpu.VMEM((2, 2, 20, 48, 128), BF16),
-    relay=pltpu.SemaphoreType.REGULAR,
     halo_send=pltpu.SemaphoreType.DMA((4,)),
     halo_recv=pltpu.SemaphoreType.DMA((4,)),
-    ar_send=pltpu.SemaphoreType.DMA((2, 6)),
-    ar_recv=pltpu.SemaphoreType.DMA((2, 6)),
+    ar_send=pltpu.SemaphoreType.DMA((2, 7)),
+    ar_recv=pltpu.SemaphoreType.DMA((2, 7)),
 )
 
 
@@ -623,8 +661,8 @@
         copy.start()
         return copy
 
-    for load in loads.values():
-        load.wait()
+    for name in ("x_in", "tab_in", "pad", "gains", "wqkv", "wproj"):
+        loads[name].wait()
     gain1, gain2 = s.gains[0:1, :], s.gains[1:2, :]
     x1 = nn(reorder("a", "n"), field(s.x_in))
     expand_first(s, lat)
@@ -632,19 +670,23 @@
     first = pack(project(s, 0, x1, s.wproj, 1), "a")
     pl.semaphore_wait(barrier, expected)
     h_first.start(first)
-    pl.semaphore_signal(s.relay, inc=1, device_id=far_peers()[2], device_id_type=MESH)
+    loads["cot_in"].wait()
     h_cot.start(pack(field(s.cot_in), "n"))
 
     expand_second(s, lat)
-    g2 = unpack(h_cot.finish(), "b").astype(BF16)
+    for i, slots in enumerate(SLOTS):
+        s.to_slots[i] = reorder(slots, "b")
+        s.from_slots[i] = reorder("b", slots)
+        s.from_slots[3 + i] = reorder("a", slots)
+    x2 = unpack(h_first.finish(), "b", [s.from_slots[i] for i in range(3)])
+    attend(s, 1, x2, gain2, s.wqkv, lambda g: s.bias2[g], 2)
+    g2 = unpack(h_cot.finish(), "b", [s.from_slots[i] for i in range(3)]).astype(BF16)
     head_backs(s, 1, g2, s.wproj, 2)
-    x2 = unpack(h_first.finish(), "b")
-    pl.semaphore_wait(s.relay, 1)
-    attend(s, 1, x2, gain2, s.wqkv, lambda g: s.bias2[g], 2)
     d_packed = backward(s, 1, 2)
     dh2, d_scaled = norm_backward(s, 1, g2, d_packed, gain2, s.wqkv)
-    h_grad.start(pack(dh2, "b"))
-    h_out.start(pack(project(s, 1, x2, s.wproj, 2), "b"))
+    h_grad.start(pack(dh2, "b", [s.to_slots[i] for i in range(3)]))
+    second = project(s, 1, x2, s.wproj, 2)
+    second = pack(second, "b", [s.to_slots[i] for i in range(3)])
     weight_gradients(s, 1, g2, d_packed, 2)
     reduce2.stages[0][0].start()
     other_gradients(s, 1, d_scaled, fold_second(s))
@@ -652,7 +694,8 @@
     h_cot.sent()
     h_first.sent()
     reduce2.step(1)
-    g1 = unpack(h_grad.finish(), "a").astype(BF16)
+    g1 = unpack(h_grad.finish(), "a", [s.from_slots[3 + i] for i in range(3)]).astype(BF16)
+    h_out.start(second)
     head_backs(s, 0, g1, s.wproj, 1)
     d_packed = backward(s, 0, 1)
     weight_gradients(s, 0, g1, d_packed, 1)
@@ -664,11 +707,11 @@
     reduce2.step(2)
     s.dx[...] = nn(reorder("n", "a"), dx).reshape(6, 12, 2, 192).astype(BF16)
     stores = [store(0, s.dx, dx_ref)]
+    h_grad.sent()
+    reduce2.step(3)
     s.out[...] = unpack(h_out.finish(), "n").reshape(6, 12, 2, 192).astype(BF16)
     stores.append(store(1, s.out, out_ref))
-    h_grad.sent()
     h_out.sent()
-    reduce2.step(3)
     reduce1.step(2)
     reduce1.step(3)
     reduce2.step(4)

time: 70.1 us -> 67.3 us (0.960)
  Pallas kernels: 69.3 us -> 66.5 us
    pallas_call x1, Pallas kernels: 66.6 us -> 63.9 us  [body(): pl.pallas_call(main_kernel, out_shape=(field, field, jax.ShapeDtypeStruct...]
where the time goes in v7:
time: 67.3 us; the launch traced here: 67.2 us
  Pallas kernels  66.5 us (99%)
    pallas_call x1, Pallas kernels, body(): pl.pallas_call(main_kernel, out_shape=(field, field, jax.ShapeDtypeStruct...  63.9 us
    pallas_call x1, Pallas kernels, body(): pl.pallas_call(finish_kernel, out_shape=(field, field, jax.ShapeDtypeStru...  2.66 us

profile of v7, /device:TPU:1, one launch (start us, length us, event | category | flops | bytes accessed | tf_op | source)
XLA Modules:
  0.0 67.2 jit_solution(17741581716700279552)
XLA Ops:
  0.6 63.9 %both_blocks.1 = (bf16[6,12,2,192]{3,2,1,0:T(2,128)(2,1)}, bf16[6,12,2,192]{3,2,1,0:T(2,128)(2,1)}, bf16[2,2,20,48,128]{4,3,2,1,0:T(8,128)(2,1)}) custom-call(bf16[6,12,2,192]{3,2,1,0:T(2,128)(2,1)} %bitcast.7, bf16[6,12,2,192]{3,2,1,0:T(2,128)(2,1)} %bitcast.8, f32[2,192]{1,0:T(2,128)} %gains_ref.1, bf16[2,192,576]{2,1,0:T(8,128)(2,1)} %wqkv_ref.1, ...), custom_call_target="tpu_custom_call" | custom-call | tf_op jit(solution)/shard_map/both_blocks/pallas_call | solution.py:772
  64.5 2.7 %unpack.1 = (bf16[6,12,2,192]{3,2,1,0:T(2,128)(2,1)}, bf16[6,12,2,192]{3,2,1,0:T(2,128)(2,1)}, f32[2,192]{1,0:T(2,128)}, f32[2,192,576]{2,1,0:T(8,128)}, f32[2,1...) custom-call(bf16[2,2,20,48,128]{4,3,2,1,0:T(8,128)(2,1)} %get-tuple-element.15.red_ref, ...), custom_call_target="tpu_custom_call" | custom-call | tf_op jit(solution)/shard_map/unpack/pallas_call | solution.py:791

commit v8 on v7

--- a/solution.py
+++ b/solution.py
@@ -467,6 +467,7 @@
         own, table = self.own, 16 + x
         near, far, half = self.near, self.far, self.half
         stages = [[] for _ in range(6)]
+        self.weight_sends, self.table_sends = [], []
 
         def add(number, src, dst, peer):
             stages[number].append(self.copy(number, src, dst, peer))
@@ -476,10 +477,12 @@
             add(0, s.payload.at[j, 1 - core, slots], s.in_core.at[j, slots], sibling())
         for i, (dx, peer, slot) in enumerate(plane_peers()):
             add(1, s.half.at[j, slot], s.in_plane.at[j, i], peer)
+            self.weight_sends.append((slot, stages[1][-1]))
             add(4, s.red.at[j, core, own], s.red.at[j, core, own], peer)
             if dx:
                 px = lax.rem(x + dx, 4)
                 add(1, s.half.at[j, 13 + px], s.in_plane.at[j, 14 + dx], peer)
+                self.table_sends.append(stages[1][-1])
                 add(4, s.red.at[j, core, table], s.red.at[j, core, table], peer)
         for peer in near_peers():
             add(2, s.near.at[j, near], s.near.at[j, near], peer)
@@ -514,9 +517,13 @@
         if number == 4:
             self.far_tab.wait_recv()
         if number == 1:
-            for slot in range(16):
+            for slot, copy in [(self.own, None)] + self.weight_sends:
                 total = s.payload[j, core, slot].astype(F32) + s.in_core[j, slot].astype(F32)
                 s.half[j, slot] = total.astype(BF16)
+                if copy is not None:
+                    copy.start()
+            for copy in self.table_sends:
+                copy.start()
         if number == 2:
             total = s.half[j, self.own].astype(F32)
             for i in range(15):
@@ -547,7 +554,7 @@
                 for copy in self.stages[3]:
                     copy.start()
 
-        elif 0 < number < 6:
+        elif 1 < number < 6:
             for copy in self.stages[number]:
                 copy.start()
         if number == 4:

time: 67.3 us -> 67.3 us (level)
  no operation moved by 1% of the time
where the time goes in v8:
time: 67.3 us; the launch traced here: 67.1 us
  Pallas kernels  66.5 us (99%)
    pallas_call x1, Pallas kernels, body(): pl.pallas_call(main_kernel, out_shape=(field, field, jax.ShapeDtypeStruct...  63.8 us
    pallas_call x1, Pallas kernels, body(): pl.pallas_call(finish_kernel, out_shape=(field, field, jax.ShapeDtypeStru...  2.66 us

profile of v8, /device:TPU:1, one launch (start us, length us, event | category | flops | bytes accessed | tf_op | source)
XLA Modules:
  0.0 67.1 jit_solution(15459458062023330435)
XLA Ops:
  0.6 63.8 %both_blocks.1 = (bf16[6,12,2,192]{3,2,1,0:T(2,128)(2,1)}, bf16[6,12,2,192]{3,2,1,0:T(2,128)(2,1)}, bf16[2,2,20,48,128]{4,3,2,1,0:T(8,128)(2,1)}) custom-call(bf16[6,12,2,192]{3,2,1,0:T(2,128)(2,1)} %bitcast.7, bf16[6,12,2,192]{3,2,1,0:T(2,128)(2,1)} %bitcast.8, f32[2,192]{1,0:T(2,128)} %gains_ref.1, bf16[2,192,576]{2,1,0:T(8,128)(2,1)} %wqkv_ref.1, ...), custom_call_target="tpu_custom_call" | custom-call | tf_op jit(solution)/shard_map/both_blocks/pallas_call | solution.py:779
  64.5 2.7 %unpack.1 = (bf16[6,12,2,192]{3,2,1,0:T(2,128)(2,1)}, bf16[6,12,2,192]{3,2,1,0:T(2,128)(2,1)}, f32[2,192]{1,0:T(2,128)}, f32[2,192,576]{2,1,0:T(8,128)}, f32[2,1...) custom-call(bf16[2,2,20,48,128]{4,3,2,1,0:T(8,128)(2,1)} %get-tuple-element.15.red_ref, ...), custom_call_target="tpu_custom_call" | custom-call | tf_op jit(solution)/shard_map/unpack/pallas_call | solution.py:798
